TPU v7x, 256 devices: a whole 4x4x8 slice. The times are simulated.
256 devices in a mesh: grp: 4 (over z_hi), gx: 32 (over x, z_lo, y), gy: 2 (over core).
Axes of the slice: x: 4, y: 4, z: 8 (z_hi: 4, z_lo: 2; z = z_hi * 2 + z_lo), core: 2. Of those that a mesh axis runs over, the one named last changes fastest.
Arguments:
- fluid_temp: float32 [512, 256, 1024], P('gx', 'gy', 'grp'), may hold values from -6 to 6
- active: int32 [512, 256, 1024], P('gx', 'gy', 'grp'), may hold values 0 or 1
- fin_temp: float32 [256, 1024, 512], P('grp', 'gx', 'gy'), may hold values from -6 to 6
- fin_source: float32 [256, 1024, 512], P('grp', 'gx', 'gy'), may hold values from -6 to 6
- wall_owner: int32 [32, 2, 2048, 1], P('gx', 'gy'), may hold values from 0 to 31, as said below
- wall_target: int32 [32, 2, 2048], P('gx', 'gy'), may hold values from 0 to 8191, as said below
Outputs:
- fluid_new: float32 [512, 256, 1024], P('gx', 'gy', 'grp')
- fin_new: float32 [256, 1024, 512], P('grp', 'gx', 'gy')
Inputs may be any that keep to these rules, and one draw needn't show every extreme that they name: `wall_owner`: among the 2048 wall cells of one column block (a, b), exactly 128 name the owner a and at most 128 name any one owner; in every draw one owner is named by exactly 128 wall cells of every column block. `wall_target`: wall cell w = i * 128 + j names a root cell (2 * i + di) * 256 + 2 * j + dj of the 2 x 2 patch beneath it, di and dj being 0 or 1; the first wall cell of a block names its patch's first root cell, the last one its patch's last.
All inputs are finite; a program needn't handle non-finite values. No bound on the sum of `active` on one device may be relied on, other than what follows from the above.
Results may differ from a plain program's by a relative error of at most 0.00002.
Values sent between devices are 32-bit elements; how exact they have to be, the bound alone decides.
A program may use at most 64 MiB of HBM per device.

v0:
```python
import jax
import jax.numpy as jnp
from jax import lax
from jax.sharding import PartitionSpec as P

FLUID_DIFFUSION = 1.0
FIN_CONDUCTION = 1.0
HEAT_COEF = 1.0


def padded_2(block, sides, width):
    for axis, dim in sides:
        count = lax.axis_size(axis)
        forward = [(i, i + 1) for i in range(count - 1)]
        backward = [(target, source) for source, target in forward]
        low = lax.ppermute(
            lax.slice_in_dim(block, block.shape[dim] - width, None, axis=dim), axis, forward
        )
        high = lax.ppermute(lax.slice_in_dim(block, 0, width, axis=dim), axis, backward)
        block = jnp.concatenate([low, block, high], axis=dim)
    return block


def six_sum(padded):
    return (
        padded[2:, 1:-1, 1:-1]
        + padded[:-2, 1:-1, 1:-1]
        + padded[1:-1, 2:, 1:-1]
        + padded[1:-1, :-2, 1:-1]
        + padded[1:-1, 1:-1, 2:]
        + padded[1:-1, 1:-1, :-2]
    )


def fin_from_padded(padded, field):
    return (1.0 + 6.0 * FIN_CONDUCTION) * field - FIN_CONDUCTION * six_sum(padded)


def fin_image(field):
    padded = padded_2(field, (("grp", 0), ("gx", 1), ("gy", 2)), 1)
    return fin_from_padded(padded, field)


def fluid_padded_apart(field):
    return padded_2(field, (("grp", 2), ("gx", 0), ("gy", 1)), 1)


def fluid_update(padded, field, fluid_temp, update_mask, ghost, on_wall):
    lowest = lax.broadcasted_iota(jnp.int32, field.shape, 2) == 0
    below = jnp.where(lowest & on_wall, ghost[:, :, None], 0.0)
    neighbours = six_sum(padded) + below
    updated = (fluid_temp + FLUID_DIFFUSION * neighbours) / (1.0 + 6.0 * FLUID_DIFFUSION)
    return jnp.where(update_mask, updated, field)


def local(fluid_temp, active, fin_temp, fin_source, wall_owner, wall_target):
    first_cells, second_cells, third_cells = fluid_temp.shape
    fin_depth, fin_width, fin_height = fin_temp.shape
    owner_count = lax.axis_size("gx")
    wall_cells = first_cells * second_cells
    capacity = min(wall_cells, max(2, 2 * wall_cells // owner_count))
    on_wall = lax.axis_index("grp") == 0
    owners = wall_owner[0, 0, :, 0]
    targets = wall_target[0, 0, :]
    onehot = (owners[:, None] == jnp.arange(owner_count, dtype=jnp.int32)[None, :]).astype(
        jnp.int32
    )
    ranks = jnp.sum((jnp.cumsum(onehot, axis=0) - onehot) * onehot, axis=1)
    slot_index = owners * capacity + ranks
    wall_temps = fluid_temp[:, :, 0].reshape(-1)
    send_temps = jnp.zeros((owner_count * capacity,), jnp.float32).at[slot_index].set(wall_temps)
    send_targets = (
        jnp.full((owner_count * capacity,), -1.0, jnp.float32)
        .at[slot_index]
        .set(targets.astype(jnp.float32))
    )
    received = lax.all_to_all(
        jnp.stack([send_temps, send_targets]), "gx", split_axis=1, concat_axis=1, tiled=True
    )
    got_targets = received[1].astype(jnp.int32)
    valid = (got_targets >= 0) & on_wall
    safe_targets = jnp.where(valid, got_targets, 0)
    surface = fin_temp[0].reshape(-1)
    fin_wall = jnp.where(valid, surface[safe_targets], 0.0)
    heat_flux = jnp.where(valid, HEAT_COEF * (received[0] - fin_wall), 0.0)
    deposit = jax.ops.segment_sum(heat_flux, safe_targets, num_segments=fin_width * fin_height)
    returned = lax.all_to_all(fin_wall, "gx", split_axis=0, concat_axis=0, tiled=True)
    ghost = returned[slot_index].reshape(first_cells, second_cells)
    fin_rhs = fin_temp + fin_source
    fin_rhs = fin_rhs.at[0].add(deposit.reshape(fin_width, fin_height))
    diag = 1.0 + 6.0 * FIN_CONDUCTION
    spectral = 6.0 * FIN_CONDUCTION / diag
    omega = 1.0 / (1.0 - spectral * spectral / 2.0)
    shape = fluid_temp.shape
    colour = (
        lax.broadcasted_iota(jnp.int32, shape, 0)
        + lax.broadcasted_iota(jnp.int32, shape, 1)
        + lax.broadcasted_iota(jnp.int32, shape, 2)
    ) % 2
    red_mask = (colour == 0) & (active == 1)
    black_mask = (colour == 1) & (active == 1)
    first_state = fin_temp + (fin_rhs - fin_image(fin_temp)) / diag
    second_image = fin_image(first_state)
    red_temp = fluid_update(
        fluid_padded_apart(fluid_temp), fluid_temp, fluid_temp, red_mask, ghost, on_wall
    )
    fluid_new = fluid_update(
        fluid_padded_apart(red_temp), red_temp, fluid_temp, black_mask, ghost, on_wall
    )
    fin_new = omega * (first_state + (fin_rhs - second_image) / diag - fin_temp) + fin_temp
    return (fluid_new, fin_new)


def solution(mesh):
    in_specs = (
        P("gx", "gy", "grp"),
        P("gx", "gy", "grp"),
        P("grp", "gx", "gy"),
        P("grp", "gx", "gy"),
        P("gx", "gy", None, None),
        P("gx", "gy", None),
    )
    out_specs = (P("gx", "gy", "grp"), P("grp", "gx", "gy"))
    return jax.shard_map(local, mesh=mesh, in_specs=in_specs, out_specs=out_specs, check_vma=False)
```

profile of v0, /device:TPU:2, one launch (start us, length us, event | category | flops | bytes accessed | tf_op | source)
XLA Modules:
  0.0 320.8 jit_solution(9975414038074076085)
XLA Ops:
  0.6 1.9 fusion.54
  4.2 9.1 %reduce-window.6 = s32[32,16,128]{2,1,0:T(8,128)S(1)} reduce-window(s32[32,16,128]{2,1,0:T(8,128)S(1)} %fusion.41, s32[]{:T(128)} %constant.65.clone.1), window={size=1x1x128 pad=0_0x0_0x127_0}, to_apply=%region_0.0 | reduce-window | flops 8323072 | bytes 524292 | tf_op jit(solution)/shard_map/reduce-window
  14.2 8.1 %scatter_custom_fusion = f32[4096]{0:T(1024)S(1)} fusion(s32[2048]{0:T(1024)S(1)} %bitcast.84, f32[2048]{0:T(1024)S(1)} %bitcast.88, f32[]{:T(128)} %constant.70.clone.1), kind=kCustom, calls=%fused_computation.160 | custom fusion | bytes 16388 | tf_op jit(solution)/shard_map/scatter | solution.py:71
  22.3 8.1 %scatter_custom_fusion.1 = f32[4096]{0:T(1024)S(1)} fusion(s32[2048]{0:T(1024)S(1)} %bitcast.85, f32[2048]{0:T(1024)S(1)} %bitcast.89, f32[]{:T(128)} %constant.73.clone.1), kind=kCustom, calls=%fused_computation.158 | custom fusion | bytes 16388 | tf_op jit(solution)/shard_map/scatter | solution.py:75
  31.0 9.0 %all-to-all-start = ((f32[2,32,128]{2,0,1:T(2,128)}), f32[2,32,128]{2,0,1:T(2,128)S(1)}, u32[]{:S(2)}, u32[]{:S(2)}) async-start(f32[2,32,128]{2,0,1:T(2,128)} %pad_maximum_fusion.88), calls=%async_computation | async-start | bytes 65536 | tf_op jit(solution)/shard_map/all_to_all | solution.py:77
  40.0 5.9 %copy_add_fusion = (f32[64,32,256]{2,0,1:T(8,128)}, f32[64,32,256]{2,0,1:T(8,128)S(1)}) fusion(f32[64,32,256]{2,1,0:T(8,128)} %param.11, f32[64,32,256]{2,1,0:T(8,128)} %param.10), kind=kLoop, calls=%fused_computation.124 | loop fusion | flops 524288 | bytes 8388608 | tf_op jit(solution)/shard_map/add | solution.py:89
  47.3 6.4 %collective-permute-start.13 = (f32[1,32,256]{2,0,1:T(1,128)S(1)}, f32[1,32,256]{2,0,1:T(1,128)S(1)}, u32[]{:S(2)}, u32[]{:S(2)}) collective-permute-start(f32[1,32,256]{2,0,1:T(1,128)S(1)} %copy.116), channel_id=1, source_target_pairs={{0,64},{64,128},{128,192},{1,65},{65,129},{129,193},{2,66},{66,130... | collective-permute-start | bytes 98312 | tf_op jit(solution)/shard_map/ppermute | solution.py:16
  54.0 6.0 %collective-permute-start = (f32[16,128,1]{1,0,2:T(8,128)S(1)}, f32[16,128,1]{1,0,2:T(8,128)S(1)}, u32[]{:S(2)}, u32[]{:S(2)}) collective-permute-start(f32[16,128,1]{1,0,2:T(8,128)S(1)} %copy.133), channel_id=1, source_target_pairs={{0,64},{64,128},{128,192},{1,65},{65,129},{129,193},{2,66},{66,130... | collective-permute-start | bytes 24584 | tf_op jit(solution)/shard_map/ppermute | solution.py:16
  60.7 1.9 copy.111
  62.6 2.9 copy.80
  66.2 5.6 %collective-permute-start.2 = (f32[1,128,258]{1,2,0:T(8,128)}, f32[1,128,258]{1,2,0:T(8,128)S(1)}, u32[]{:S(2)}, u32[]{:S(2)}) collective-permute-start(f32[1,128,258]{1,2,0:T(8,128)} %get-tuple-element.41), channel_id=1, source_target_pairs={{2,0},{4,2},{6,4},{8,6},{10,8},{12,10},{14,12},{16,14},{18,16},{20... | collective-permute-start | bytes 396296 | tf_op jit(solution)/shard_map/ppermute | solution.py:19
  71.8 1.9 collective-permute-start.3
  73.8 6.9 %collective-permute-start.14 = (f32[66,1,256]{2,0,1:T(8,128)S(1)}, f32[66,1,256]{2,0,1:T(8,128)S(1)}, u32[]{:S(2)}, u32[]{:S(2)}) collective-permute-start(f32[66,1,256]{2,0,1:T(8,128)S(1)} %get-tuple-element.37), channel_id=1, source_target_pairs={{2,0},{4,2},{6,4},{8,6},{10,8},{12,10},{14,12},{16,14},{18,16},{20... | collective-permute-start | bytes 202760 | tf_op jit(solution)/shard_map/ppermute | solution.py:19
  80.7 1.9 collective-permute-start.15
  82.8 23.0 %gather_fusion = f32[4096]{0:T(1024)S(1)} fusion(f32[8192]{0:T(1024)S(1)} %bitcast.54, s32[4096]{0:T(1024)S(1)} %broadcast_clamp_fusion), kind=kCustom, calls=%fused_computation | custom fusion | bytes 49152 | tf_op jit(solution)/shard_map/gather | solution.py:84
  106.5 9.5 %all-to-all-start.1 = ((f32[32,128,1]{1,2,0:T(1,128)}), f32[32,128,1]{1,2,0:T(1,128)S(1)}, u32[]{:S(2)}, u32[]{:S(2)}) async-start(f32[32,128,1]{1,2,0:T(1,128)} %bitcast.19), calls=%async_computation.1 | async-start | bytes 32768 | tf_op jit(solution)/shard_map/all_to_all | solution.py:87
  115.9 28.3 %scatter_custom_fusion.2 = f32[8192]{0:T(1024)} fusion(s32[4096]{0:T(1024)S(1)} %bitcast.87, f32[4096]{0:T(1024)S(1)} %get-tuple-element.20, f32[]{:T(128)} %constant.70.clone.1), kind=kCustom, calls=%fused_computation.153 | custom fusion | flops 4096 | bytes 32772 | tf_op jit(solution)/shard_map/scatter-add | solution.py:86
  145.5 1.8 pad_maximum_fusion
  148.7 2.4 copy.119
  153.6 4.2 %collective-permute-start.17 = (f32[66,34,1]{0,1,2:T(8,128)}, f32[66,34,1]{0,1,2:T(8,128)}, u32[]{:S(2)}, u32[]{:S(2)}) collective-permute-start(f32[66,34,1]{0,1,2:T(8,128)} %copy.121), channel_id=1, source_target_pairs={{0,1},{2,3},{4,5},{6,7},{8,9},{10,11},{12,13},{14,15},{16,17},{18,... | collective-permute-start | bytes 26936 | tf_op jit(solution)/shard_map/ppermute | solution.py:16
  160.6 11.9 %gather_fusion.1 = f32[2048]{0:T(1024)S(1)} fusion(f32[4096]{0:T(1024)S(1)} %bitcast.55, s32[2048]{0:T(1024)} %broadcast_clamp_fusion.1), kind=kCustom, calls=%fused_computation.1 | custom fusion | bytes 24576 | tf_op jit(solution)/shard_map/gather | solution.py:88
  173.8 2.3 copy.122
  176.0 13.9 %fusion.23 = f32[64,32,256]{2,0,1:T(8,128)} fusion(f32[64,32,256]{2,0,1:T(8,128)} %copy-done.1, f32[64,32,256]{2,0,1:T(8,128)} %scatter-add.13, f32[66,34,1]{2,0,1:T(8,128)} %copy.122, f32[66,1,256]{2,0,1:T(8,128)} %copy-done.7, f32[66,1,256]{2,0,1:T(8,128)} %copy-done.8, f32[1,32,256]{2,0,1:T(1,128)S(1)} %collective-permute-done.12, ...), kind=kLoop, calls=%fused_computation.56 | loop fusion | flops 14680064 | bytes 6510112 | tf_op jit(solution)/shard_map/add | solution.py:102
  191.1 2.9 fusion.51
  194.0 3.0 copy.86
  198.3 3.0 copy.88
  201.4 3.0 collective-permute-start.5
  206.8 6.6 %collective-permute-start.19 = (f32[1,32,256]{2,0,1:T(1,128)S(1)}, f32[1,32,256]{2,0,1:T(1,128)S(1)}, u32[]{:S(2)}, u32[]{:S(2)}) collective-permute-start(f32[1,32,256]{2,0,1:T(1,128)S(1)} %get-tuple-element.42), channel_id=1, source_target_pairs={{0,64},{64,128},{128,192},{1,65},{65,129},{129,193},{2,66},{66,130... | collective-permute-start | bytes 98312 | tf_op jit(solution)/shard_map/ppermute | solution.py:16
  213.4 2.3 copy.87
  215.7 2.2 copy.89
  217.9 8.2 %fusion.2 = (f32[16,128,256]{1,2,0:T(8,128)S(1)}, pred[16,128,256]{1,2,0:T(8,128)(4,1)}) fusion(f32[16,128,256]{1,2,0:T(8,128)S(1)} %copy.111, f32[16,128,1]{1,2,0:T(1,128)S(1)} %bitcast.65, f32[16,128,1]{1,2,0:T(1,128)S(1)} %bitcast.62, f32[18,1,258]{1,2,0:T(8,128)} %copy.89, f32[1,128,258]{1,2,0:T(8,128)S(1)} %collective-permute-done.2, ...), kind=kLoop, calls=%fused_computation.16 | loop fusion | flops 23068672 | bytes 7141920 | tf_op jit(solution)/shard_map/jit(_where)/select_n | solution.py:53
  226.2 6.0 %collective-permute-start.6 = (f32[16,128,1]{1,0,2:T(8,128)S(1)}, f32[16,128,1]{1,0,2:T(8,128)S(1)}, u32[]{:S(2)}, u32[]{:S(2)}) collective-permute-start(f32[16,128,1]{1,0,2:T(8,128)S(1)} %bitcast.91), channel_id=1, source_target_pairs={{0,64},{64,128},{128,192},{1,65},{65,129},{129,193},{2,66},{66,130... | collective-permute-start | bytes 24584 | tf_op jit(solution)/shard_map/ppermute | solution.py:16
  233.6 5.5 %collective-permute-start.20 = (f32[66,1,256]{2,0,1:T(8,128)S(1)}, f32[66,1,256]{2,0,1:T(8,128)S(1)}, u32[]{:S(2)}, u32[]{:S(2)}) collective-permute-start(f32[66,1,256]{2,0,1:T(8,128)S(1)} %get-tuple-element.35), channel_id=1, source_target_pairs={{2,0},{4,2},{6,4},{8,6},{10,8},{12,10},{14,12},{16,14},{18,16},{20... | collective-permute-start | bytes 202760 | tf_op jit(solution)/shard_map/ppermute | solution.py:19
  239.1 1.9 collective-permute-start.21
  241.8 6.9 %collective-permute-start.8 = (f32[1,128,258]{1,2,0:T(8,128)}, f32[1,128,258]{1,2,0:T(8,128)S(1)}, u32[]{:S(2)}, u32[]{:S(2)}) collective-permute-start(f32[1,128,258]{1,2,0:T(8,128)} %get-tuple-element.39), channel_id=1, source_target_pairs={{2,0},{4,2},{6,4},{8,6},{10,8},{12,10},{14,12},{16,14},{18,16},{20... | collective-permute-start | bytes 396296 | tf_op jit(solution)/shard_map/ppermute | solution.py:19
  248.7 1.9 collective-permute-start.9
  257.9 4.2 %collective-permute-start.23 = (f32[66,34,1]{0,1,2:T(8,128)}, f32[66,34,1]{0,1,2:T(8,128)}, u32[]{:S(2)}, u32[]{:S(2)}) collective-permute-start(f32[66,34,1]{0,1,2:T(8,128)} %copy.126), channel_id=1, source_target_pairs={{0,1},{2,3},{4,5},{6,7},{8,9},{10,11},{12,13},{14,15},{16,17},{18,... | collective-permute-start | bytes 26936 | tf_op jit(solution)/shard_map/ppermute | solution.py:16
  263.4 2.4 copy.127
  267.6 3.0 fusion.50
  270.6 3.7 %copy.105 = f32[18,1,258]{2,0,1:T(8,128)} copy(f32[18,1,258]{1,2,0:T(8,128)} %get-tuple-element.30) | data formatting | bytes 37152 | tf_op jit(solution)/shard_map/slice | solution.py:19
  275.5 3.7 %copy.107 = f32[18,1,258]{2,0,1:T(8,128)} copy(f32[18,1,258]{1,2,0:T(8,128)} %get-tuple-element.31) | data formatting | bytes 37152 | tf_op jit(solution)/shard_map/slice | solution.py:17
  279.2 4.2 %collective-permute-start.11 = (f32[18,1,258]{2,0,1:T(8,128)}, f32[18,1,258]{2,0,1:T(8,128)}, u32[]{:S(2)}, u32[]{:S(2)}) collective-permute-start(f32[18,1,258]{2,0,1:T(8,128)} %copy.107), channel_id=1, source_target_pairs={{0,1},{2,3},{4,5},{6,7},{8,9},{10,11},{12,13},{14,15},{16,17},{18,... | collective-permute-start | bytes 55736 | tf_op jit(solution)/shard_map/ppermute | solution.py:16
  283.4 14.3 %fusion.14 = f32[64,32,256]{2,0,1:T(8,128)S(1)} fusion(f32[64,32,256]{2,0,1:T(8,128)} %fusion.23, f32[64,32,256]{2,0,1:T(8,128)} %scatter-add.13, f32[66,34,1]{2,0,1:T(8,128)} %copy.127, f32[66,1,256]{2,0,1:T(8,128)} %copy-done.9, f32[66,1,256]{2,0,1:T(8,128)} %copy-done.10, f32[1,32,256]{2,0,1:T(1,128)S(1)} %collective-permute-done.18, ...), kind=kLoop, calls=%fused_computation.29 | loop fusion | flops 16252928 | bytes 8607264 | tf_op jit(solution)/shard_map/add | solution.py:110
  297.8 2.5 copy.131
  300.3 3.0 copy.106
  303.4 3.1 copy.108
  306.5 11.5 %fusion.5 = f32[16,128,256]{1,2,0:T(8,128)} fusion(f32[16,128,256]{1,2,0:T(8,128)} %copy-done.3, f32[16,128,256]{1,2,0:T(8,128)S(1)} %copy.111, f32[16,128,1]{1,2,0:T(1,128)S(1)} %bitcast.68, f32[16,128,1]{1,2,0:T(1,128)S(1)} %bitcast.71, f32[18,1,258]{1,2,0:T(8,128)} %copy.108, f32[1,128,258]{1,2,0:T(8,128)S(1)} %collective-permute-done.8, ...), kind=kLoop, calls=%fused_computation.19 | loop fusion | flops 22544384 | bytes 7141920 | tf_op jit(solution)/shard_map/jit(_where)/select_n | solution.py:53
  317.9 2.9 copy.130
  (109 shorter events, 34.5 us)
Async XLA Ops:
  0.6 3.6 %copy-start.11 = (s32[1,1,2048,1]{2,3,1,0:T(1,128)S(1)}, s32[1,1,2048,1]{2,3,1,0:T(1,128)}, u32[]{:S(2)}) copy-start(s32[1,1,2048,1]{2,3,1,0:T(1,128)} %param.12) | copy-start | bytes 24580
  2.5 11.6 %copy-start.14 = (s32[1,1,2048]{2,1,0:T(1,128)S(1)}, s32[1,1,2048]{2,1,0:T(1,128)}, u32[]{:S(2)}) copy-start(s32[1,1,2048]{2,1,0:T(1,128)} %param.13) | copy-start | bytes 24580
  2.9 62.6 %collective-permute-start.1 = (f32[16,128,1]{1,0,2:T(8,128)S(1)}, f32[16,128,1]{1,0,2:T(8,128)S(1)}, u32[]{:S(2)}, u32[]{:S(2)}) collective-permute-start(f32[16,128,1]{1,0,2:T(8,128)S(1)} %copy.134), channel_id=1, source_target_pairs={{64,0},{128,64},{192,128},{65,1},{129,65},{193,129},{66,2},{130,66... | collective-permute-start | bytes 24584 | tf_op jit(solution)/shard_map/ppermute | solution.py:19
  31.0 51.7 %all-to-all-start = ((f32[2,32,128]{2,0,1:T(2,128)}), f32[2,32,128]{2,0,1:T(2,128)S(1)}, u32[]{:S(2)}, u32[]{:S(2)}) async-start(f32[2,32,128]{2,0,1:T(2,128)} %pad_maximum_fusion.88), calls=%async_computation | async-start | bytes 65536 | tf_op jit(solution)/shard_map/all_to_all | solution.py:77
  40.0 7.2 %slice-start = ((f32[64,32,256]{2,1,0:T(8,128)}), f32[1,32,256]{2,1,0:T(8,128)S(1)}, s32[]{:S(2)}) async-start(f32[64,32,256]{2,1,0:T(8,128)} %param.10), calls=%async_computation.2 | async-start | bytes 65536 | tf_op jit(solution)/shard_map/slice | solution.py:17
  45.9 14.8 %copy-start.1 = (f32[64,32,256]{2,0,1:T(8,128)}, f32[64,32,256]{2,0,1:T(8,128)S(1)}, u32[]{:S(2)}) copy-start(f32[64,32,256]{2,0,1:T(8,128)S(1)} %get-tuple-element.45) | copy-start | bytes 6291460
  45.9 27.8 %collective-permute-start.12 = (f32[1,32,256]{2,0,1:T(1,128)S(1)}, f32[1,32,256]{2,0,1:T(1,128)S(1)}, u32[]{:S(2)}, u32[]{:S(2)}) collective-permute-start(f32[1,32,256]{2,0,1:T(1,128)S(1)} %slice.268), channel_id=1, source_target_pairs={{64,0},{128,64},{192,128},{65,1},{129,65},{193,129},{66,2},{130,66... | collective-permute-start | bytes 98312 | tf_op jit(solution)/shard_map/ppermute | solution.py:19
  47.3 26.5 %collective-permute-start.13 = (f32[1,32,256]{2,0,1:T(1,128)S(1)}, f32[1,32,256]{2,0,1:T(1,128)S(1)}, u32[]{:S(2)}, u32[]{:S(2)}) collective-permute-start(f32[1,32,256]{2,0,1:T(1,128)S(1)} %copy.116), channel_id=1, source_target_pairs={{0,64},{64,128},{128,192},{1,65},{65,129},{129,193},{2,66},{66,130... | collective-permute-start | bytes 98312 | tf_op jit(solution)/shard_map/ppermute | solution.py:16
  54.0 11.5 %collective-permute-start = (f32[16,128,1]{1,0,2:T(8,128)S(1)}, f32[16,128,1]{1,0,2:T(8,128)S(1)}, u32[]{:S(2)}, u32[]{:S(2)}) collective-permute-start(f32[16,128,1]{1,0,2:T(8,128)S(1)} %copy.133), channel_id=1, source_target_pairs={{0,64},{64,128},{128,192},{1,65},{65,129},{129,193},{2,66},{66,130... | collective-permute-start | bytes 24584 | tf_op jit(solution)/shard_map/ppermute | solution.py:16
  60.7 157.2 %copy-start.15 = (pred[256]{0:T(512)(128)(4,1)}, pred[256]{0:T(512)(128)(4,1)S(1)}, u32[]{:S(2)}) copy-start(pred[256]{0:T(512)(128)(4,1)S(1)} %compare_and_fusion.1) | copy-start | bytes 772
  65.5 8.3 %copy-start.2 = (f32[64,32,256]{2,0,1:T(8,128)S(1)}, f32[64,32,256]{2,0,1:T(8,128)}, u32[]{:S(2)}) copy-start(f32[64,32,256]{2,0,1:T(8,128)} %copy-done.1) | copy-start | bytes 6291460
  66.2 123.7 %collective-permute-start.2 = (f32[1,128,258]{1,2,0:T(8,128)}, f32[1,128,258]{1,2,0:T(8,128)S(1)}, u32[]{:S(2)}, u32[]{:S(2)}) collective-permute-start(f32[1,128,258]{1,2,0:T(8,128)} %get-tuple-element.41), channel_id=1, source_target_pairs={{2,0},{4,2},{6,4},{8,6},{10,8},{12,10},{14,12},{16,14},{18,16},{20... | collective-permute-start | bytes 396296 | tf_op jit(solution)/shard_map/ppermute | solution.py:19
  71.8 118.2 %collective-permute-start.3 = (f32[1,128,258]{1,2,0:T(8,128)}, f32[1,128,258]{1,2,0:T(8,128)}, u32[]{:S(2)}, u32[]{:S(2)}) collective-permute-start(f32[1,128,258]{1,2,0:T(8,128)} %get-tuple-element.40), channel_id=1, source_target_pairs={{0,2},{2,4},{4,6},{6,8},{8,10},{10,12},{12,14},{14,16},{16,18},{18... | collective-permute-start | bytes 396296 | tf_op jit(solution)/shard_map/ppermute | solution.py:16
  73.8 70.5 %copy-start.5 = (f32[1,32,256]{2,0,1:T(1,128)}, f32[1,32,256]{2,0,1:T(1,128)S(1)}, u32[]{:S(2)}) copy-start(f32[1,32,256]{2,0,1:T(1,128)S(1)} %collective-permute-done.13) | copy-start | bytes 98308
  73.8 70.4 %collective-permute-start.14 = (f32[66,1,256]{2,0,1:T(8,128)S(1)}, f32[66,1,256]{2,0,1:T(8,128)S(1)}, u32[]{:S(2)}, u32[]{:S(2)}) collective-permute-start(f32[66,1,256]{2,0,1:T(8,128)S(1)} %get-tuple-element.37), channel_id=1, source_target_pairs={{2,0},{4,2},{6,4},{8,6},{10,8},{12,10},{14,12},{16,14},{18,16},{20... | collective-permute-start | bytes 202760 | tf_op jit(solution)/shard_map/ppermute | solution.py:19
  80.7 63.5 %collective-permute-start.15 = (f32[66,1,256]{2,0,1:T(8,128)S(1)}, f32[66,1,256]{2,0,1:T(8,128)S(1)}, u32[]{:S(2)}, u32[]{:S(2)}) collective-permute-start(f32[66,1,256]{2,0,1:T(8,128)S(1)} %get-tuple-element.36), channel_id=1, source_target_pairs={{0,2},{2,4},{4,6},{6,8},{8,10},{10,12},{12,14},{14,16},{16,18},{18... | collective-permute-start | bytes 202760 | tf_op jit(solution)/shard_map/ppermute | solution.py:16
  106.5 54.1 %all-to-all-start.1 = ((f32[32,128,1]{1,2,0:T(1,128)}), f32[32,128,1]{1,2,0:T(1,128)S(1)}, u32[]{:S(2)}, u32[]{:S(2)}) async-start(f32[32,128,1]{1,2,0:T(1,128)} %bitcast.19), calls=%async_computation.1 | async-start | bytes 32768 | tf_op jit(solution)/shard_map/all_to_all | solution.py:87
  144.2 0.6 copy-start.7
  144.8 0.6 copy-start.8
  151.2 21.3 %collective-permute-start.16 = (f32[66,34,1]{0,1,2:T(8,128)}, f32[66,34,1]{0,1,2:T(8,128)}, u32[]{:S(2)}, u32[]{:S(2)}) collective-permute-start(f32[66,34,1]{0,1,2:T(8,128)} %copy.119), channel_id=1, source_target_pairs={{1,0},{3,2},{5,4},{7,6},{9,8},{11,10},{13,12},{15,14},{17,16},{19,... | collective-permute-start | bytes 26936 | tf_op jit(solution)/shard_map/ppermute | solution.py:19
  153.6 20.2 %collective-permute-start.17 = (f32[66,34,1]{0,1,2:T(8,128)}, f32[66,34,1]{0,1,2:T(8,128)}, u32[]{:S(2)}, u32[]{:S(2)}) collective-permute-start(f32[66,34,1]{0,1,2:T(8,128)} %copy.121), channel_id=1, source_target_pairs={{0,1},{2,3},{4,5},{6,7},{8,9},{10,11},{12,13},{14,15},{16,17},{18,... | collective-permute-start | bytes 26936 | tf_op jit(solution)/shard_map/ppermute | solution.py:16
  172.5 45.4 %copy-start.12 = (f32[2048]{0:T(1024)}, f32[2048]{0:T(1024)S(1)}, u32[]{:S(2)}) copy-start(f32[2048]{0:T(1024)S(1)} %gather_fusion.1) | copy-start | bytes 24580
  197.0 16.3 %collective-permute-start.4 = (f32[18,1,258]{2,0,1:T(8,128)S(1)}, f32[18,1,258]{2,0,1:T(8,128)S(1)}, u32[]{:S(2)}, u32[]{:S(2)}) collective-permute-start(f32[18,1,258]{2,0,1:T(8,128)S(1)} %copy.86), channel_id=1, source_target_pairs={{1,0},{3,2},{5,4},{7,6},{9,8},{11,10},{13,12},{15,14},{17,16},{19,... | collective-permute-start | bytes 55736 | tf_op jit(solution)/shard_map/ppermute | solution.py:19
  201.4 14.3 %collective-permute-start.5 = (f32[18,1,258]{2,0,1:T(8,128)S(1)}, f32[18,1,258]{2,0,1:T(8,128)S(1)}, u32[]{:S(2)}, u32[]{:S(2)}) collective-permute-start(f32[18,1,258]{2,0,1:T(8,128)S(1)} %copy.88), channel_id=1, source_target_pairs={{0,1},{2,3},{4,5},{6,7},{8,9},{10,11},{12,13},{14,15},{16,17},{18,... | collective-permute-start | bytes 55736 | tf_op jit(solution)/shard_map/ppermute | solution.py:16
  205.5 28.0 %collective-permute-start.18 = (f32[1,32,256]{2,0,1:T(1,128)S(1)}, f32[1,32,256]{2,0,1:T(1,128)S(1)}, u32[]{:S(2)}, u32[]{:S(2)}) collective-permute-start(f32[1,32,256]{2,0,1:T(1,128)S(1)} %get-tuple-element.43), channel_id=1, source_target_pairs={{64,0},{128,64},{192,128},{65,1},{129,65},{193,129},{66,2},{130,66... | collective-permute-start | bytes 98312 | tf_op jit(solution)/shard_map/ppermute | solution.py:19
  206.8 26.7 %collective-permute-start.19 = (f32[1,32,256]{2,0,1:T(1,128)S(1)}, f32[1,32,256]{2,0,1:T(1,128)S(1)}, u32[]{:S(2)}, u32[]{:S(2)}) collective-permute-start(f32[1,32,256]{2,0,1:T(1,128)S(1)} %get-tuple-element.42), channel_id=1, source_target_pairs={{0,64},{64,128},{128,192},{1,65},{65,129},{129,193},{2,66},{66,130... | collective-permute-start | bytes 98312 | tf_op jit(solution)/shard_map/ppermute | solution.py:16
  217.9 15.6 %copy-start = (f32[64,32,256]{2,0,1:T(8,128)S(1)}, f32[64,32,256]{2,0,1:T(8,128)}, u32[]{:S(2)}) copy-start(f32[64,32,256]{2,0,1:T(8,128)} %fusion.23) | copy-start | bytes 6291460
  226.1 15.6 %copy-start.3 = (f32[16,128,256]{1,2,0:T(8,128)}, f32[16,128,256]{1,2,0:T(8,128)S(1)}, u32[]{:S(2)}) copy-start(f32[16,128,256]{1,2,0:T(8,128)S(1)} %get-tuple-element.22) | copy-start | bytes 6291460
  226.2 14.8 %collective-permute-start.6 = (f32[16,128,1]{1,0,2:T(8,128)S(1)}, f32[16,128,1]{1,0,2:T(8,128)S(1)}, u32[]{:S(2)}, u32[]{:S(2)}) collective-permute-start(f32[16,128,1]{1,0,2:T(8,128)S(1)} %bitcast.91), channel_id=1, source_target_pairs={{0,64},{64,128},{128,192},{1,65},{65,129},{129,193},{2,66},{66,130... | collective-permute-start | bytes 24584 | tf_op jit(solution)/shard_map/ppermute | solution.py:16
  232.2 8.8 %collective-permute-start.7 = (f32[16,128,1]{1,0,2:T(8,128)S(1)}, f32[16,128,1]{1,0,2:T(8,128)S(1)}, u32[]{:S(2)}, u32[]{:S(2)}) collective-permute-start(f32[16,128,1]{1,0,2:T(8,128)S(1)} %bitcast.90), channel_id=1, source_target_pairs={{64,0},{128,64},{192,128},{65,1},{129,65},{193,129},{66,2},{130,66... | collective-permute-start | bytes 24584 | tf_op jit(solution)/shard_map/ppermute | solution.py:19
  233.5 17.1 %copy-start.6 = (f32[1,32,256]{2,0,1:T(1,128)}, f32[1,32,256]{2,0,1:T(1,128)S(1)}, u32[]{:S(2)}) copy-start(f32[1,32,256]{2,0,1:T(1,128)S(1)} %collective-permute-done.19) | copy-start | bytes 98308
  233.6 17.1 %collective-permute-start.20 = (f32[66,1,256]{2,0,1:T(8,128)S(1)}, f32[66,1,256]{2,0,1:T(8,128)S(1)}, u32[]{:S(2)}, u32[]{:S(2)}) collective-permute-start(f32[66,1,256]{2,0,1:T(8,128)S(1)} %get-tuple-element.35), channel_id=1, source_target_pairs={{2,0},{4,2},{6,4},{8,6},{10,8},{12,10},{14,12},{16,14},{18,16},{20... | collective-permute-start | bytes 202760 | tf_op jit(solution)/shard_map/ppermute | solution.py:19
  239.1 11.6 %collective-permute-start.21 = (f32[66,1,256]{2,0,1:T(8,128)S(1)}, f32[66,1,256]{2,0,1:T(8,128)S(1)}, u32[]{:S(2)}, u32[]{:S(2)}) collective-permute-start(f32[66,1,256]{2,0,1:T(8,128)S(1)} %get-tuple-element.34), channel_id=1, source_target_pairs={{0,2},{2,4},{4,6},{6,8},{8,10},{10,12},{12,14},{14,16},{16,18},{18... | collective-permute-start | bytes 202760 | tf_op jit(solution)/shard_map/ppermute | solution.py:16
  241.8 24.0 %collective-permute-start.8 = (f32[1,128,258]{1,2,0:T(8,128)}, f32[1,128,258]{1,2,0:T(8,128)S(1)}, u32[]{:S(2)}, u32[]{:S(2)}) collective-permute-start(f32[1,128,258]{1,2,0:T(8,128)} %get-tuple-element.39), channel_id=1, source_target_pairs={{2,0},{4,2},{6,4},{8,6},{10,8},{12,10},{14,12},{16,14},{18,16},{20... | collective-permute-start | bytes 396296 | tf_op jit(solution)/shard_map/ppermute | solution.py:19
  248.7 17.1 %collective-permute-start.9 = (f32[1,128,258]{1,2,0:T(8,128)}, f32[1,128,258]{1,2,0:T(8,128)}, u32[]{:S(2)}, u32[]{:S(2)}) collective-permute-start(f32[1,128,258]{1,2,0:T(8,128)} %get-tuple-element.38), channel_id=1, source_target_pairs={{0,2},{2,4},{4,6},{6,8},{8,10},{10,12},{12,14},{14,16},{16,18},{18... | collective-permute-start | bytes 396296 | tf_op jit(solution)/shard_map/ppermute | solution.py:16
  250.6 0.6 copy-start.9
  251.3 0.6 copy-start.10
  255.5 6.7 %collective-permute-start.22 = (f32[66,34,1]{0,1,2:T(8,128)S(1)}, f32[66,34,1]{0,1,2:T(8,128)}, u32[]{:S(2)}, u32[]{:S(2)}) collective-permute-start(f32[66,34,1]{0,1,2:T(8,128)S(1)} %copy.124), channel_id=1, source_target_pairs={{1,0},{3,2},{5,4},{7,6},{9,8},{11,10},{13,12},{15,14},{17,16},{19,... | collective-permute-start | bytes 26936 | tf_op jit(solution)/shard_map/ppermute | solution.py:19
  257.9 5.5 %collective-permute-start.23 = (f32[66,34,1]{0,1,2:T(8,128)}, f32[66,34,1]{0,1,2:T(8,128)}, u32[]{:S(2)}, u32[]{:S(2)}) collective-permute-start(f32[66,34,1]{0,1,2:T(8,128)} %copy.126), channel_id=1, source_target_pairs={{0,1},{2,3},{4,5},{6,7},{8,9},{10,11},{12,13},{14,15},{16,17},{18,... | collective-permute-start | bytes 26936 | tf_op jit(solution)/shard_map/ppermute | solution.py:16
  274.2 26.1 %collective-permute-start.10 = (f32[18,1,258]{2,0,1:T(8,128)}, f32[18,1,258]{2,0,1:T(8,128)}, u32[]{:S(2)}, u32[]{:S(2)}) collective-permute-start(f32[18,1,258]{2,0,1:T(8,128)} %copy.105), channel_id=1, source_target_pairs={{1,0},{3,2},{5,4},{7,6},{9,8},{11,10},{13,12},{15,14},{17,16},{19,... | collective-permute-start | bytes 55736 | tf_op jit(solution)/shard_map/ppermute | solution.py:19
  279.2 24.2 %collective-permute-start.11 = (f32[18,1,258]{2,0,1:T(8,128)}, f32[18,1,258]{2,0,1:T(8,128)}, u32[]{:S(2)}, u32[]{:S(2)}) collective-permute-start(f32[18,1,258]{2,0,1:T(8,128)} %copy.107), channel_id=1, source_target_pairs={{0,1},{2,3},{4,5},{6,7},{8,9},{10,11},{12,13},{14,15},{16,17},{18,... | collective-permute-start | bytes 55736 | tf_op jit(solution)/shard_map/ppermute | solution.py:16
  300.3 6.1 %copy-start.4 = (pred[16,128,256]{1,2,0:T(8,128)(4,1)S(1)}, pred[16,128,256]{1,2,0:T(8,128)(4,1)}, u32[]{:S(2)}) copy-start(pred[16,128,256]{1,2,0:T(8,128)(4,1)} %get-tuple-element.23) | copy-start | bytes 1572868
  300.3 6.1 %copy-start.13 = (f32[2048]{0:T(1024)S(1)}, f32[2048]{0:T(1024)}, u32[]{:S(2)}) copy-start(f32[2048]{0:T(1024)} %copy-done.12) | copy-start | bytes 24580
  300.3 6.1 %copy-start.16 = (pred[256]{0:T(512)(128)(4,1)S(1)}, pred[256]{0:T(512)(128)(4,1)}, u32[]{:S(2)}) copy-start(pred[256]{0:T(512)(128)(4,1)} %copy-done.15) | copy-start | bytes 772
where the time goes:
time: 323 us; the launch traced here: 321 us
  local copies, waits for them, and re-layouts  116 us (36%)
  starting transfers between devices  102 us (32%)
  other arithmetic  101 us (31%)
    ppermute x12, starting transfers between devices, padded_2(): lax.ppermute(lax.slice_in_dim(block, block.shape[dim] - width, None, axis...  48.4 us
    ppermute x12, starting transfers between devices, padded_2(): lax.ppermute(lax.slice_in_dim(block, 0, width, axis=dim), axis, backward)  35.3 us
    scatter-add x1, other arithmetic, local(): jax.ops.segment_sum(heat_flux, safe_targets, num_segments=fin_width * fin...  28.3 us
    gather x1, local copies, waits for them, and re-layouts, local(): fin_wall = jnp.where(valid, surface[safe_targets], 0.0)  23 us
    slice x10, local copies, waits for them, and re-layouts, padded_2(): lax.slice_in_dim(block, 0, width, axis=dim)  21.7 us
    select_n x2, other arithmetic, fluid_update(): return jnp.where(update_mask, updated, field)  19.7 us
    add x1, other arithmetic, local(): omega * (first_state + (fin_rhs - second_image) / diag - fin_temp)  14.3 us
    add x1, other arithmetic, local(): first_state = fin_temp + (fin_rhs - fin_image(fin_temp)) / diag  13.9 us
  transfers between devices with their start and end apart: 26, of which 0 were waited for; matrix products, arithmetic and copies ran while one was open for 56% of the time, Pallas kernels for 0%

commit v1 on v0

v1 whole, which is shorter than its diff:
```python
import functools

import jax
import jax.numpy as jnp
from jax import lax
from jax.experimental import pallas as pl
from jax.experimental.pallas import tpu as pltpu
from jax.sharding import PartitionSpec as P

F32 = jnp.float32
MESH = pl.DeviceIdType.MESH
DIAG = 7.0
SPECTRAL = 6.0 / DIAG
OMEGA = 1.0 / (1.0 - SPECTRAL * SPECTRAL / 2.0)
SEVENTH = 1.0 / 7.0

CX, CY, CZ = 16, 128, 256
FD, FW, FH = 64, 32, 256
ROWS = CX

FLUID_UP, FLUID_DOWN, FLUID_SIDE, FLUID_ABOVE, FLUID_BELOW = 0, 1, 2, 3, 4
FIN_UP, FIN_DOWN, FIN_SIDE, FIN_ABOVE, FIN_BELOW = 5, 6, 7, 8, 9
FACES = 10


def iota(shape, axis):
    return lax.broadcasted_iota(jnp.int32, shape, axis)


def parity_rows(shape):
    rows, lanes = shape
    tile = (iota((8, lanes), 0) + iota((8, lanes), 1)) % 2
    return jnp.concatenate([tile] * (rows // 8), axis=0)


def shifted_rows(plane, low_tile, high_tile):
    rows, lanes = plane.shape
    sub = iota((8, lanes), 0)
    up = pltpu.roll(plane, 1, 0)
    down = pltpu.roll(plane, rows - 1, 0)
    up = jnp.concatenate([jnp.where(sub == 0, low_tile, up[:8]), up[8:]], axis=0)
    down = jnp.concatenate([down[:-8], jnp.where(sub == 7, high_tile, down[-8:])], axis=0)
    return up + down


def shifted_lanes(plane, low_tile, high_tile):
    rows, lanes = plane.shape
    lane = iota((rows, 128), 1)
    left = pltpu.roll(plane, 1, 1)
    right = pltpu.roll(plane, lanes - 1, 1)
    first = jnp.where(lane == 0, low_tile, left[:, :128]) + right[:, :128]
    last = left[:, 128:] + jnp.where(lane == 127, high_tile, right[:, 128:])
    return jnp.concatenate([first, last], axis=1)


def fluid_plane(x, field, active, side, low, high, parity, core):
    here = field[x + 1]
    total = field[x] + field[x + 2]
    tile = side[x]
    low_tile = jnp.where(core == 1, pltpu.roll(tile, 1, 0), 0.0)
    high_tile = jnp.where(core == 0, pltpu.roll(tile, 7, 0), 0.0)
    total = total + shifted_rows(here, low_tile, high_tile)
    low_lane = pltpu.roll(low[...], (128 - x) % 128, 1)
    high_lane = pltpu.roll(high[...], 127 - x, 1)
    total = total + shifted_lanes(here, low_lane, high_lane)
    on = jnp.where(parity_rows(here.shape) == (x + parity) % 2, active[x], 0) == 1
    return jnp.where(on, (here + total) * SEVENTH, here)


def fin_sum(group, k, field, low, high, side, core):
    d = group * 8 + k
    here = field[d + 1]
    total = field[d] + field[d + 2]
    low_tile = pltpu.roll(low[group], (8 - k) % 8, 0)
    high_tile = pltpu.roll(high[group], 7 - k, 0)
    total = total + shifted_rows(here, low_tile, high_tile)
    column = pltpu.roll(side[...], jnp.where(core == 1, (128 - d) % 128, 127 - d), 1)
    total = total + shifted_lanes(
        here, jnp.where(core == 1, column, 0.0), jnp.where(core == 0, column, 0.0)
    )
    return here, total


def pick_columns(x, plane, low, high):
    lane = iota((plane.shape[0], 128), 1)
    low[...] = jnp.where(lane == x, pltpu.roll(plane[:, :128], x, 1), low[...])
    high[...] = jnp.where(lane == x, pltpu.roll(plane[:, 128:], (x + 1) % 128, 1), high[...])


def pick_rows(k, plane, low, high):
    sub = iota((8, plane.shape[1]), 0)
    low = jnp.where(sub == k, pltpu.roll(plane[:8], k, 0), low)
    high = jnp.where(sub == k, pltpu.roll(plane[-8:], (k + 1) % 8, 0), high)
    return low, high


def pick_side(d, plane, out, core):
    lane = iota((plane.shape[0], 128), 1)
    half = jnp.where(core == 0, plane[:, 128:], plane[:, :128])
    turned = pltpu.roll(half, jnp.where(core == 0, (d + 1) % 128, d), 1)
    out[...] = jnp.where(lane == d, turned, out[...])


def spread(rows, columns, offset, axis):
    a, b = iota((rows, columns), axis), iota((rows, columns), 1 - axis)
    return jnp.where(a == 2 * b + offset, 1.0, 0.0).astype(F32)


def dot(a, b):
    return jnp.dot(a, b, precision=lax.Precision.HIGHEST, preferred_element_type=F32)


def exchange_kernel(
    sizes,
    fluid, active, fin, source, owner, target,
    red, active_v, first, base, side2, low2, high2, fin_low2, fin_high2, fin_side2,
    fluid_v, fin_v, source_v, owner_v, target_v,
    side1, low1, high1, fin_low1, fin_high1, fin_side1,
    out_low1, out_high1, out_fin_low1, out_fin_high1, out_fin_side1,
    out_low2, out_high2, out_fin_low2, out_fin_high2, out_fin_side2,
    wall_out, wall_in, back_out, back_in,
    load_sem, send1, recv1, send2, recv2, wall_send, wall_recv, back_send, back_recv,
):
    groups, blocks = sizes
    grp, gx, core = lax.axis_index("grp"), lax.axis_index("gx"), lax.axis_index("gy")
    has_low, has_high = gx > 0, gx < blocks - 1
    has_below, has_above = grp > 0, grp < groups - 1
    on_wall = grp == 0
    left, right = (grp, gx - 1, core), (grp, gx + 1, core)
    below, above = (grp - 1, gx, core), (grp + 1, gx, core)
    other = (grp, gx, 1 - core)

    def peer(k):
        return (grp, lax.rem(gx + k, blocks), core)

    def peer_back(k):
        return (grp, lax.rem(gx - k + blocks, blocks), core)

    loads = [
        pltpu.make_async_copy(owner, owner_v, load_sem.at[0]),
        pltpu.make_async_copy(target, target_v, load_sem.at[1]),
        pltpu.make_async_copy(fluid, fluid_v.at[pl.ds(1, CX)], load_sem.at[2]),
        pltpu.make_async_copy(fin, fin_v.at[pl.ds(1, FD)], load_sem.at[3]),
        pltpu.make_async_copy(active, active_v, load_sem.at[4]),
        pltpu.make_async_copy(source, source_v, load_sem.at[5]),
    ]
    for load in loads:
        load.start()

    barrier = pltpu.get_barrier_semaphore()

    def greet(device):
        pl.semaphore_signal(barrier, inc=1, device_id=device, device_id_type=MESH)

    greet(other)

    @pl.when(has_above)
    def _():
        greet(above)

    @pl.when(has_below)
    def _():
        greet(below)

    @pl.when(on_wall)
    def _():
        def step(k, carry):
            greet(peer(k))
            return carry

        lax.fori_loop(1, blocks, step, 0)

    @pl.when(jnp.logical_not(on_wall) & has_low)
    def _():
        greet(left)

    @pl.when(jnp.logical_not(on_wall) & has_high)
    def _():
        greet(right)

    @pl.when(jnp.logical_not(has_low))
    def _():
        fluid_v[0] = jnp.zeros((CY, CZ), F32)
        red[0] = jnp.zeros((CY, CZ), F32)
        fin_low1[...] = jnp.zeros(fin_low1.shape, F32)
        fin_low2[...] = jnp.zeros(fin_low2.shape, F32)

    @pl.when(jnp.logical_not(has_high))
    def _():
        fluid_v[CX + 1] = jnp.zeros((CY, CZ), F32)
        red[CX + 1] = jnp.zeros((CY, CZ), F32)
        fin_high1[...] = jnp.zeros(fin_high1.shape, F32)
        fin_high2[...] = jnp.zeros(fin_high2.shape, F32)

    @pl.when(jnp.logical_not(has_below))
    def _():
        low1[...] = jnp.zeros(low1.shape, F32)

    @pl.when(jnp.logical_not(has_above))
    def _():
        high1[...] = jnp.zeros(high1.shape, F32)
        high2[...] = jnp.zeros(high2.shape, F32)
        fin_v[FD + 1] = jnp.zeros((FW, FH), F32)
        first[FD + 1] = jnp.zeros((FW, FH), F32)

    for ref in (out_low1, out_high1, out_fin_side1, out_low2, out_high2, out_fin_side2):
        ref[...] = jnp.zeros(ref.shape, F32)

    loads[0].wait()
    loads[1].wait()
    loads[2].wait()

    def pack_fluid(x, carry):
        pick_columns(x, fluid_v[x + 1], out_low1, out_high1)
        return carry

    lax.fori_loop(0, CX, pack_fluid, 0)

    expected = 1 + has_above.astype(jnp.int32) + has_below.astype(jnp.int32)
    sides = has_low.astype(jnp.int32) + has_high.astype(jnp.int32)
    pl.semaphore_wait(barrier, expected + jnp.where(on_wall, blocks - 1, sides))

    def link(src, dst, send, recv, k, device):
        return pltpu.make_async_remote_copy(
            src_ref=src, dst_ref=dst, send_sem=send.at[k], recv_sem=recv.at[k],
            device_id=device, device_id_type=MESH,
        )

    def wall_link(k):
        return link(wall_out.at[k], wall_in.at[k], wall_send, wall_recv, k, peer(k))

    def back_link(k):
        return link(back_out.at[k], back_in.at[k], back_send, back_recv, k, peer_back(k))

    @pl.when(on_wall)
    def _():
        temps = jnp.transpose(out_low1[...])[:ROWS]
        owners = owner_v[...]
        targets = target_v[...].astype(F32)

        def masked(k, out):
            out[k, :ROWS] = temps
            out[k, ROWS:] = jnp.where(owners == lax.rem(gx + k, blocks), targets, -1.0)

        def step(k, carry):
            masked(k, wall_out)
            wall_link(k).start()
            return carry

        masked(0, wall_in)
        lax.fori_loop(1, blocks, step, 0)

    side_row = pl.multiple_of(jnp.where(core == 0, CY - 8, 0), 8)

    def faces(send, recv, fluid_from, fluid_off, fluid_to, side, low, high, sent_low, sent_high,
              fin_from, fin_off, fin_to, fin_low, fin_high, fin_side, sent_fin_low, sent_fin_high, sent_fin_side):
        return {
            FLUID_UP: (link(fluid_from.at[CX - 1 + fluid_off], fluid_to.at[0], send, recv, FLUID_UP, right), has_high, has_low),
            FLUID_DOWN: (link(fluid_from.at[fluid_off], fluid_to.at[CX + 1], send, recv, FLUID_DOWN, left), has_low, has_high),
            FLUID_SIDE: (link(fluid_from.at[pl.ds(fluid_off, CX), pl.ds(side_row, 8)], side, send, recv, FLUID_SIDE, other), None, None),
            FLUID_ABOVE: (link(sent_high, low, send, recv, FLUID_ABOVE, above), has_above, has_below),
            FLUID_BELOW: (link(sent_low, high, send, recv, FLUID_BELOW, below), has_below, has_above),
            FIN_UP: (link(sent_fin_high, fin_low, send, recv, FIN_UP, right), has_high, has_low),
            FIN_DOWN: (link(sent_fin_low, fin_high, send, recv, FIN_DOWN, left), has_low, has_high),
            FIN_SIDE: (link(sent_fin_side, fin_side, send, recv, FIN_SIDE, other), None, None),
            FIN_ABOVE: (link(fin_from.at[FD - 1 + fin_off], fin_to.at[0], send, recv, FIN_ABOVE, above), has_above, has_below),
            FIN_BELOW: (link(fin_from.at[fin_off], fin_to.at[FD + 1], send, recv, FIN_BELOW, below), has_below, has_above),
        }

    def when(condition, action):
        if condition is None:
            action()
        else:
            pl.when(condition)(action)

    one = faces(send1, recv1, fluid, 0, fluid_v, side1, low1, high1, out_low1, out_high1,
                fin, 0, fin_v, fin_low1, fin_high1, fin_side1, out_fin_low1, out_fin_high1, out_fin_side1)
    two = faces(send2, recv2, red, 1, red, side2, low2, high2, out_low2, out_high2,
                first, 1, first, fin_low2, fin_high2, fin_side2, out_fin_low2, out_fin_high2, out_fin_side2)

    def start(links, *which):
        for k in which:
            when(links[k][1], links[k][0].start)

    def arrived(links, *which):
        for k in which:
            when(links[k][2], links[k][0].wait_recv)

    def sent(links):
        for k in range(FACES):
            when(links[k][1], links[k][0].wait_send)

    start(one, FLUID_SIDE, FLUID_ABOVE, FLUID_BELOW, FIN_ABOVE, FIN_BELOW, FLUID_UP, FLUID_DOWN)

    loads[3].wait()

    def pack_fin(group, carry):
        low = high = jnp.zeros((8, FH), F32)
        for k in range(8):
            plane = fin_v[group * 8 + k + 1]
            low, high = pick_rows(k, plane, low, high)
            pick_side(group * 8 + k, plane, out_fin_side1, core)
        out_fin_low1[group] = low
        out_fin_high1[group] = high
        return carry

    lax.fori_loop(0, FD // 8, pack_fin, 0)
    start(one, FIN_SIDE, FIN_UP, FIN_DOWN)

    loads[4].wait()
    loads[5].wait()
    arrived(one, FLUID_SIDE, FLUID_ABOVE, FLUID_BELOW)

    def red_step(x, carry):
        new = fluid_plane(x, fluid_v, active_v, side1, low1, high1, 0, core)
        red[x + 1] = new
        pick_columns(x, new, out_low2, out_high2)
        return carry

    lax.fori_loop(1, CX - 1, red_step, 0)
    arrived(one, FLUID_UP, FLUID_DOWN)
    red_step(0, 0)
    red_step(CX - 1, 0)

    arrived(one, FIN_SIDE, FIN_UP, FIN_DOWN, FIN_BELOW)

    def fin_step(group, carry):
        low = high = jnp.zeros((8, FH), F32)
        for k in range(8):
            d = group * 8 + k
            here, total = fin_sum(group, k, fin_v, fin_low1, fin_high1, fin_side1, core)
            rhs = here + source_v[d]
            new = (rhs + total) * SEVENTH
            first[d + 1] = new
            base[d] = (OMEGA * SEVENTH) * rhs + (1.0 - OMEGA) * here
            low, high = pick_rows(k, new, low, high)
            pick_side(d, new, out_fin_side2, core)
        out_fin_low2[group] = low
        out_fin_high2[group] = high
        return carry

    lax.fori_loop(1, FD // 8, fin_step, 0)

    arrived(one, FIN_ABOVE)

    @pl.when(on_wall)
    def _():
        cells = (ROWS, CY)
        least = (2 * FH * iota(cells, 0) + 2 * iota(cells, 1)).astype(F32)
        roots = fin_v[1]
        surface = []
        for di in range(2):
            for dj in range(2):
                columns = dot(roots, spread(FH, CY, dj, 0))
                surface.append(dot(spread(ROWS, FW, di, 1), columns))
        shifts = (0.0, 1.0, float(FH), float(FH + 1))

        def owned(k, sums):
            offset = wall_in[k, ROWS:] - least
            temps = wall_in[k, :ROWS]
            value = jnp.zeros(cells, F32)
            new = []
            for part, shift, total in zip(surface, shifts, sums):
                hit = offset == shift
                value = jnp.where(hit, part, value)
                new.append(total + jnp.where(hit, temps - part, 0.0))
            back_out[k] = value
            return tuple(new)

        def step(k, sums):
            wall_link(k).wait_recv()
            sums = owned(k, sums)
            back_link(k).start()
            return sums

        sums = owned(0, (jnp.zeros(cells, F32),) * 4)
        sums = lax.fori_loop(1, blocks, step, sums)
        deposit = jnp.zeros((FW, FH), F32)
        for di in range(2):
            rows = spread(FW, ROWS, di, 0)
            for dj in range(2):
                deposit = deposit + dot(
                    dot(rows, sums[2 * di + dj]), spread(CY, FH, dj, 1)
                )
        fin_v[0] = deposit
        first[0] = deposit

    fin_step(0, 0)

    @pl.when(on_wall)
    def _():
        def step(k, total):
            back_link(k).wait_recv()
            return total + back_in[k]

        ghost = lax.fori_loop(1, blocks, step, back_out[0])
        square = jnp.concatenate([ghost, jnp.zeros((CY - ROWS, CY), F32)], axis=0)
        low2[...] = jnp.transpose(square)

        def fix(x, carry):
            lane = iota((CY, 128), 1)
            on = jnp.where(parity_rows((CY, 128)) == x % 2, active_v[x, :, :128], 0) == 1
            share = pltpu.roll(low2[...], (128 - x) % 128, 1) * SEVENTH
            half = red[x + 1, :, :128]
            red[x + 1, :, :128] = half + jnp.where(on & (lane == 0), share, 0.0)
            return carry

        lax.fori_loop(0, CX, fix, 0)

    start(two, FLUID_UP, FLUID_DOWN, FLUID_SIDE, FLUID_ABOVE, FLUID_BELOW,
          FIN_UP, FIN_DOWN, FIN_SIDE, FIN_ABOVE, FIN_BELOW)

    sent(one)

    @pl.when(on_wall)
    def _():
        def step(k, carry):
            wall_link(k).wait_send()
            back_link(k).wait_send()
            return carry

        lax.fori_loop(1, blocks, step, 0)

    arrived(two, *range(FACES))
    sent(two)


def second_kernel(
    red, active, first, base, side, low, high, fin_low, fin_high, fin_side,
    fluid_out, fin_out, fluid_v, fin_v, fluid_sem, fin_sem,
):
    core = lax.axis_index("gy")

    def fluid_copy(x):
        return pltpu.make_async_copy(fluid_v.at[x], fluid_out.at[x], fluid_sem.at[x])

    def fin_copy(group):
        part = pl.ds(group * 8, 8)
        return pltpu.make_async_copy(fin_v.at[part], fin_out.at[part], fin_sem.at[group])

    def black_step(x, carry):
        fluid_v[x] = fluid_plane(x, red, active, side, low, high, 1, core)
        fluid_copy(x).start()
        return carry

    lax.fori_loop(0, CX, black_step, 0)

    def fin_step(group, carry):
        for k in range(8):
            d = group * 8 + k
            _, total = fin_sum(group, k, first, fin_low, fin_high, fin_side, core)
            fin_v[d] = base[d] + (OMEGA * SEVENTH) * total
        fin_copy(group).start()
        return carry

    lax.fori_loop(0, FD // 8, fin_step, 0)

    def fluid_done(x, carry):
        fluid_copy(x).wait()
        return carry

    def fin_done(group, carry):
        fin_copy(group).wait()
        return carry

    lax.fori_loop(0, CX, fluid_done, 0)
    lax.fori_loop(0, FD // 8, fin_done, 0)


def local(sizes, fluid_temp, active, fin_temp, fin_source, wall_owner, wall_target):
    blocks = sizes[1]
    owner = wall_owner.reshape(CX, CY)
    target = wall_target.reshape(CX, CY)
    anywhere = pl.BlockSpec(memory_space=pl.ANY)
    vmem = pl.BlockSpec(memory_space=pltpu.VMEM)
    column, rows, strip = (CY, 128), (FD // 8, 8, FH), (FW, 128)
    shapes = [
        (CX + 2, CY, CZ), None, (FD + 2, FW, FH), (FD, FW, FH),
        (CX, 8, CZ), column, column, rows, rows, strip,
    ]
    held = [
        pltpu.VMEM((CX, CY, CZ), jnp.int32) if s is None else pltpu.VMEM(s, F32) for s in shapes
    ]
    dma = pltpu.SemaphoreType.DMA
    middle = pl.pallas_call(
        functools.partial(exchange_kernel, sizes),
        name="exchange_and_first_sweeps",
        out_shape=held,
        in_specs=[anywhere] * 6,
        out_specs=[vmem] * 10,
        scratch_shapes=[
            pltpu.VMEM((CX + 2, CY, CZ), F32),
            pltpu.VMEM((FD + 2, FW, FH), F32),
            pltpu.VMEM((FD, FW, FH), F32),
            pltpu.VMEM((CX, CY), jnp.int32),
            pltpu.VMEM((CX, CY), jnp.int32),
            pltpu.VMEM((CX, 8, CZ), F32),
            *[pltpu.VMEM(s, F32) for s in (column, column, rows, rows, strip)],
            *[pltpu.VMEM(s, F32) for s in (column, column, rows, rows, strip)],
            *[pltpu.VMEM(s, F32) for s in (column, column, rows, rows, strip)],
            pltpu.VMEM((blocks, 2 * ROWS, CY), F32),
            pltpu.VMEM((blocks, 2 * ROWS, CY), F32),
            pltpu.VMEM((blocks, ROWS, CY), F32),
            pltpu.VMEM((blocks, ROWS, CY), F32),
            dma((6,)),
            *[dma((FACES,)) for _ in range(4)],
            *[dma((blocks,)) for _ in range(4)],
        ],
        compiler_params=pltpu.CompilerParams(
            collective_id=0, has_side_effects=True, vmem_limit_bytes=40 * 2**20
        ),
    )(fluid_temp, active, fin_temp, fin_source, owner, target)
    return pl.pallas_call(
        second_kernel,
        name="second_sweeps",
        out_shape=[
            jax.ShapeDtypeStruct((CX, CY, CZ), F32),
            jax.ShapeDtypeStruct((FD, FW, FH), F32),
        ],
        in_specs=[vmem] * 10,
        out_specs=[anywhere] * 2,
        scratch_shapes=[
            pltpu.VMEM((CX, CY, CZ), F32),
            pltpu.VMEM((FD, FW, FH), F32),
            dma((CX,)),
            dma((FD // 8,)),
        ],
        compiler_params=pltpu.CompilerParams(vmem_limit_bytes=40 * 2**20),
    )(*middle)


def solution(mesh):
    in_specs = (
        P("gx", "gy", "grp"),
        P("gx", "gy", "grp"),
        P("grp", "gx", "gy"),
        P("grp", "gx", "gy"),
        P("gx", "gy", None, None),
        P("gx", "gy", None),
    )
    out_specs = (P("gx", "gy", "grp"), P("grp", "gx", "gy"))
    sizes = (mesh.shape["grp"], mesh.shape["gx"])
    body = functools.partial(local, sizes)
    return jax.shard_map(body, mesh=mesh, in_specs=in_specs, out_specs=out_specs, check_vma=False)
```

time: 323 us -> 52.3 us (0.16)
  the two profiles are of different devices: /device:TPU:2 before, /device:TPU:32 now
where the time goes in v1:
time: 52.3 us; the launch traced here: 52.1 us
  Pallas kernels  46.9 us (90%)
  local copies, waits for them, and re-layouts  4.57 us (9%)
  between operations  0.65 us (1%)
    pallas_call x1, Pallas kernels, local(): pl.pallas_call(functools.partial(exchange_kernel, sizes), name='exchange_...  40.8 us
    pallas_call x1, Pallas kernels, local(): pl.pallas_call(second_kernel, name='second_sweeps', out_shape=[jax.ShapeD...  6.04 us
    unnamed x8, local copies, waits for them, and re-layouts  4.57 us

profile of v1, /device:TPU:32, one launch (start us, length us, event | category | flops | bytes accessed | tf_op | source)
XLA Modules:
  0.0 52.1 jit_solution(4934156636063923251)
XLA Ops:
  0.6 0.0 copy-start
  0.6 1.6 %copy-done = f32[16,128,256]{2,1,0:T(8,128)S(1)} copy-done((f32[16,128,256]{2,1,0:T(8,128)S(1)}, f32[16,128,256]{2,1,0:T(8,128)}, u32[]{:S(2)}) %copy-start) | copy-done | bytes 2097176
  2.2 0.0 copy-start.1
  2.2 1.6 %copy-done.1 = s32[16,128,256]{2,1,0:T(8,128)S(1)} copy-done((s32[16,128,256]{2,1,0:T(8,128)S(1)}, s32[16,128,256]{2,1,0:T(8,128)}, u32[]{:S(2)}) %copy-start.1) | copy-done | bytes 2097176
  3.8 0.0 copy-start.2
  3.8 0.7 %copy-done.2 = s32[1,1,2048,1]{2,3,1,0:T(1,128)S(1)} copy-done((s32[1,1,2048,1]{2,3,1,0:T(1,128)S(1)}, s32[1,1,2048,1]{2,3,1,0:T(1,128)}, u32[]{:S(2)}) %copy-start.2) | copy-done | bytes 8216
  4.5 0.0 copy-start.3
  4.5 0.7 %copy-done.3 = s32[1,1,2048]{2,1,0:T(1,128)S(1)} copy-done((s32[1,1,2048]{2,1,0:T(1,128)S(1)}, s32[1,1,2048]{2,1,0:T(1,128)}, u32[]{:S(2)}) %copy-start.3) | copy-done | bytes 8216
  5.2 40.8 %exchange_and_first_sweeps.1 = (f32[18,128,256]{2,1,0:T(8,128)S(1)}, s32[16,128,256]{2,1,0:T(8,128)S(1)}, f32[66,32,256]{2,1,0:T(8,128)S(1)}, f32[64,32,256]{2,1...) custom-call(f32[16,128,256]{2,1,0:T(8,128)S(1)} %copy-done, ...), custom_call_target="tpu_custom_call" | custom-call | tf_op jit(solution)/shard_map/exchange_and_first_sweeps/pallas_call | solution.py:485
  46.1 6.0 %second_sweeps.1 = (f32[16,128,256]{2,1,0:T(8,128)}, f32[64,32,256]{2,1,0:T(8,128)}) custom-call(f32[18,128,256]{2,1,0:T(8,128)S(1)} %get-tuple-element.12.red, s32[16,128,256]{2,1,0:T(8,128)S(1)} %get-tuple-element.13.active, f32[66,32,256]{2,1,0:T(8,128)S(1)} %get-tuple-element.14.first, f32[64,32,256]{2,1,0:T(8,128)S(1)} %get-tuple-element.15.base, ...), custom_call_target="tpu_custom_call" | custom-call | tf_op jit(solution)/shard_map/second_sweeps/pallas_call | solution.py:513
Async XLA Ops:
  0.6 1.6 %copy-start = (f32[16,128,256]{2,1,0:T(8,128)S(1)}, f32[16,128,256]{2,1,0:T(8,128)}, u32[]{:S(2)}) copy-start(f32[16,128,256]{2,1,0:T(8,128)} %fluid.1) | copy-start | bytes 6291460
  2.2 1.6 %copy-start.1 = (s32[16,128,256]{2,1,0:T(8,128)S(1)}, s32[16,128,256]{2,1,0:T(8,128)}, u32[]{:S(2)}) copy-start(s32[16,128,256]{2,1,0:T(8,128)} %active.1) | copy-start | bytes 6291460
  3.8 0.7 %copy-start.2 = (s32[1,1,2048,1]{2,3,1,0:T(1,128)S(1)}, s32[1,1,2048,1]{2,3,1,0:T(1,128)}, u32[]{:S(2)}) copy-start(s32[1,1,2048,1]{2,3,1,0:T(1,128)} %param.10) | copy-start | bytes 24580
  4.5 0.7 %copy-start.3 = (s32[1,1,2048]{2,1,0:T(1,128)S(1)}, s32[1,1,2048]{2,1,0:T(1,128)}, u32[]{:S(2)}) copy-start(s32[1,1,2048]{2,1,0:T(1,128)} %param.11) | copy-start | bytes 24580

commit v2 on v1

--- a/solution.py
+++ b/solution.py
@@ -18,9 +18,12 @@
 FD, FW, FH = 64, 32, 256
 ROWS = CX
 
-FLUID_UP, FLUID_DOWN, FLUID_SIDE, FLUID_ABOVE, FLUID_BELOW = 0, 1, 2, 3, 4
-FIN_UP, FIN_DOWN, FIN_SIDE, FIN_ABOVE, FIN_BELOW = 5, 6, 7, 8, 9
-FACES = 10
+HALF = CY // 2
+
+FLUID_UP, FLUID_DOWN, FLUID_SIDE = (0, 1), (2, 3), (4, 5)
+FLUID_ABOVE, FLUID_BELOW = 6, 7
+FIN_UP, FIN_DOWN, FIN_SIDE, FIN_ABOVE, FIN_BELOW = 8, 9, 10, 11, 12
+FACES = 13
 
 
 def iota(shape, axis):
@@ -87,6 +90,24 @@
     high[...] = jnp.where(lane == x, pltpu.roll(plane[:, 128:], (x + 1) % 128, 1), high[...])
 
 
+def one_colour(plane, colour):
+    folded = pltpu.roll(plane[HALF:], HALF - 1, 0)
+    return jnp.where(parity_rows(folded.shape) == colour, plane[:HALF], folded)
+
+
+def both_halves(folded):
+    return jnp.concatenate([folded, pltpu.roll(folded, 1, 0)], axis=0)
+
+
+def as_rows(columns):
+    return jnp.transpose(columns)[:ROWS]
+
+
+def as_columns(rows):
+    square = jnp.concatenate([rows, jnp.zeros((CY - ROWS, CY), F32)], axis=0)
+    return jnp.transpose(square)
+
+
 def pick_rows(k, plane, low, high):
     sub = iota((8, plane.shape[1]), 0)
     low = jnp.where(sub == k, pltpu.roll(plane[:8], k, 0), low)
@@ -116,8 +137,10 @@
     red, active_v, first, base, side2, low2, high2, fin_low2, fin_high2, fin_side2,
     fluid_v, fin_v, source_v, owner_v, target_v,
     side1, low1, high1, fin_low1, fin_high1, fin_side1,
-    out_low1, out_high1, out_fin_low1, out_fin_high1, out_fin_side1,
-    out_low2, out_high2, out_fin_low2, out_fin_high2, out_fin_side2,
+    out_fin_low1, out_fin_high1, out_fin_side1, out_fin_low2, out_fin_high2, out_fin_side2,
+    low_column, high_column,
+    out_low1, out_high1, in_low1, in_high1, out_low2, out_high2, in_low2, in_high2,
+    out_up1, out_down1, in_up1, in_down1, out_up2, out_down2, in_up2, in_down2,
     wall_out, wall_in, back_out, back_in,
     load_sem, send1, recv1, send2, recv2, wall_send, wall_recv, back_send, back_recv,
 ):
@@ -194,16 +217,16 @@
 
     @pl.when(jnp.logical_not(has_below))
     def _():
-        low1[...] = jnp.zeros(low1.shape, F32)
+        in_low1[...] = jnp.zeros(in_low1.shape, F32)
 
     @pl.when(jnp.logical_not(has_above))
     def _():
-        high1[...] = jnp.zeros(high1.shape, F32)
-        high2[...] = jnp.zeros(high2.shape, F32)
+        in_high1[...] = jnp.zeros(in_high1.shape, F32)
+        in_high2[...] = jnp.zeros(in_high2.shape, F32)
         fin_v[FD + 1] = jnp.zeros((FW, FH), F32)
         first[FD + 1] = jnp.zeros((FW, FH), F32)
 
-    for ref in (out_low1, out_high1, out_fin_side1, out_low2, out_high2, out_fin_side2):
+    for ref in (low_column, high_column, out_fin_side1, out_fin_side2):
         ref[...] = jnp.zeros(ref.shape, F32)
 
     loads[0].wait()
@@ -211,10 +234,19 @@
     loads[2].wait()
 
     def pack_fluid(x, carry):
-        pick_columns(x, fluid_v[x + 1], out_low1, out_high1)
+        pick_columns(x, fluid_v[x + 1], low_column, high_column)
         return carry
 
     lax.fori_loop(0, CX, pack_fluid, 0)
+    out_low1[...] = as_rows(low_column[...])
+    out_high1[...] = as_rows(high_column[...])
+
+    def fold(field, x, colour, out, half):
+        out[half] = one_colour(field[x + 1, :, half * 128 : half * 128 + 128], colour)
+
+    for half in range(2):
+        fold(fluid_v, CX - 1, 0, out_up1, half)
+        fold(fluid_v, 0, 1, out_down1, half)
 
     expected = 1 + has_above.astype(jnp.int32) + has_below.astype(jnp.int32)
     sides = has_low.astype(jnp.int32) + has_high.astype(jnp.int32)
@@ -234,7 +266,7 @@
 
     @pl.when(on_wall)
     def _():
-        temps = jnp.transpose(out_low1[...])[:ROWS]
+        temps = out_low1[...]
         owners = owner_v[...]
         targets = target_v[...].astype(F32)
 
@@ -252,20 +284,25 @@
 
     side_row = pl.multiple_of(jnp.where(core == 0, CY - 8, 0), 8)
 
-    def faces(send, recv, fluid_from, fluid_off, fluid_to, side, low, high, sent_low, sent_high,
-              fin_from, fin_off, fin_to, fin_low, fin_high, fin_side, sent_fin_low, sent_fin_high, sent_fin_side):
-        return {
-            FLUID_UP: (link(fluid_from.at[CX - 1 + fluid_off], fluid_to.at[0], send, recv, FLUID_UP, right), has_high, has_low),
-            FLUID_DOWN: (link(fluid_from.at[fluid_off], fluid_to.at[CX + 1], send, recv, FLUID_DOWN, left), has_low, has_high),
-            FLUID_SIDE: (link(fluid_from.at[pl.ds(fluid_off, CX), pl.ds(side_row, 8)], side, send, recv, FLUID_SIDE, other), None, None),
-            FLUID_ABOVE: (link(sent_high, low, send, recv, FLUID_ABOVE, above), has_above, has_below),
-            FLUID_BELOW: (link(sent_low, high, send, recv, FLUID_BELOW, below), has_below, has_above),
+    def faces(send, recv, side_from, out_up, in_up, out_down, in_down, side, out_low, in_low, out_high, in_high,
+              fin_from, fin_to, fin_low, fin_high, fin_side, sent_fin_low, sent_fin_high, sent_fin_side):
+        links = {
+            FLUID_ABOVE: (link(out_high, in_low, send, recv, FLUID_ABOVE, above), has_above, has_below),
+            FLUID_BELOW: (link(out_low, in_high, send, recv, FLUID_BELOW, below), has_below, has_above),
             FIN_UP: (link(sent_fin_high, fin_low, send, recv, FIN_UP, right), has_high, has_low),
             FIN_DOWN: (link(sent_fin_low, fin_high, send, recv, FIN_DOWN, left), has_low, has_high),
             FIN_SIDE: (link(sent_fin_side, fin_side, send, recv, FIN_SIDE, other), None, None),
-            FIN_ABOVE: (link(fin_from.at[FD - 1 + fin_off], fin_to.at[0], send, recv, FIN_ABOVE, above), has_above, has_below),
-            FIN_BELOW: (link(fin_from.at[fin_off], fin_to.at[FD + 1], send, recv, FIN_BELOW, below), has_below, has_above),
+            FIN_ABOVE: (link(fin_from.at[FD], fin_to.at[0], send, recv, FIN_ABOVE, above), has_above, has_below),
+            FIN_BELOW: (link(fin_from.at[1], fin_to.at[FD + 1], send, recv, FIN_BELOW, below), has_below, has_above),
         }
+        for half in range(2):
+            up, down, across = FLUID_UP[half], FLUID_DOWN[half], FLUID_SIDE[half]
+            lanes = pl.ds(half * 128, 128)
+            rim = side_from.at[pl.ds(1, CX), pl.ds(side_row, 8), lanes]
+            links[up] = (link(out_up.at[half], in_up.at[half], send, recv, up, right), has_high, has_low)
+            links[down] = (link(out_down.at[half], in_down.at[half], send, recv, down, left), has_low, has_high)
+            links[across] = (link(rim, side.at[:, :, lanes], send, recv, across, other), None, None)
+        return links
 
     def when(condition, action):
         if condition is None:
@@ -273,10 +310,10 @@
         else:
             pl.when(condition)(action)
 
-    one = faces(send1, recv1, fluid, 0, fluid_v, side1, low1, high1, out_low1, out_high1,
-                fin, 0, fin_v, fin_low1, fin_high1, fin_side1, out_fin_low1, out_fin_high1, out_fin_side1)
-    two = faces(send2, recv2, red, 1, red, side2, low2, high2, out_low2, out_high2,
-                first, 1, first, fin_low2, fin_high2, fin_side2, out_fin_low2, out_fin_high2, out_fin_side2)
+    one = faces(send1, recv1, fluid_v, out_up1, in_up1, out_down1, in_down1, side1, out_low1, in_low1, out_high1, in_high1,
+                fin_v, fin_v, fin_low1, fin_high1, fin_side1, out_fin_low1, out_fin_high1, out_fin_side1)
+    two = faces(send2, recv2, red, out_up2, in_up2, out_down2, in_down2, side2, out_low2, in_low2, out_high2, in_high2,
+                first, first, fin_low2, fin_high2, fin_side2, out_fin_low2, out_fin_high2, out_fin_side2)
 
     def start(links, *which):
         for k in which:
@@ -290,9 +327,10 @@
         for k in range(FACES):
             when(links[k][1], links[k][0].wait_send)
 
-    start(one, FLUID_SIDE, FLUID_ABOVE, FLUID_BELOW, FIN_ABOVE, FIN_BELOW, FLUID_UP, FLUID_DOWN)
+    start(one, *FLUID_UP, *FLUID_DOWN, *FLUID_SIDE, FLUID_ABOVE, FLUID_BELOW)
 
     loads[3].wait()
+    start(one, FIN_ABOVE, FIN_BELOW)
 
     def pack_fin(group, carry):
         low = high = jnp.zeros((8, FH), F32)
@@ -309,20 +347,83 @@
 
     loads[4].wait()
     loads[5].wait()
-    arrived(one, FLUID_SIDE, FLUID_ABOVE, FLUID_BELOW)
+    arrived(one, *FLUID_SIDE, FLUID_ABOVE, FLUID_BELOW)
+    low1[...] = as_columns(in_low1[...])
+    high1[...] = as_columns(in_high1[...])
 
     def red_step(x, carry):
         new = fluid_plane(x, fluid_v, active_v, side1, low1, high1, 0, core)
         red[x + 1] = new
-        pick_columns(x, new, out_low2, out_high2)
+        pick_columns(x, new, low_column, high_column)
         return carry
 
     lax.fori_loop(1, CX - 1, red_step, 0)
-    arrived(one, FLUID_UP, FLUID_DOWN)
+
+    @pl.when(on_wall)
+    def _():
+        cells = (ROWS, CY)
+        least = (2 * FH * iota(cells, 0) + 2 * iota(cells, 1)).astype(F32)
+        roots = fin_v[1]
+        surface = []
+        for di in range(2):
+            for dj in range(2):
+                columns = dot(roots, spread(FH, CY, dj, 0))
+                surface.append(dot(spread(ROWS, FW, di, 1), columns))
+        shifts = (0.0, 1.0, float(FH), float(FH + 1))
+
+        def owned(k, sums):
+            offset = wall_in[k, ROWS:] - least
+            temps = wall_in[k, :ROWS]
+            value = jnp.zeros(cells, F32)
+            new = []
+            for part, shift, total in zip(surface, shifts, sums):
+                hit = offset == shift
+                value = jnp.where(hit, part, value)
+                new.append(total + jnp.where(hit, temps - part, 0.0))
+            back_out[k] = value
+            return tuple(new)
+
+        def step(k, sums):
+            wall_link(k).wait_recv()
+            sums = owned(k, sums)
+            back_link(k).start()
+            return sums
+
+        sums = owned(0, (jnp.zeros(cells, F32),) * 4)
+        sums = lax.fori_loop(1, blocks, step, sums)
+        deposit = jnp.zeros((FW, FH), F32)
+        for di in range(2):
+            rows = spread(FW, ROWS, di, 0)
+            for dj in range(2):
+                deposit = deposit + dot(
+                    dot(rows, sums[2 * di + dj]), spread(CY, FH, dj, 1)
+                )
+        fin_v[0] = deposit
+        first[0] = deposit
+
+    def unfold(arrived_up, arrived_down, field):
+        def low_plane():
+            for half in range(2):
+                field[0, :, half * 128 : half * 128 + 128] = both_halves(arrived_up[half])
+
+        def high_plane():
+            for half in range(2):
+                field[CX + 1, :, half * 128 : half * 128 + 128] = both_halves(arrived_down[half])
+
+        when(has_low, low_plane)
+        when(has_high, high_plane)
+
+    arrived(one, *FLUID_UP, *FLUID_DOWN)
+    unfold(in_up1, in_down1, fluid_v)
     red_step(0, 0)
     red_step(CX - 1, 0)
-
-    arrived(one, FIN_SIDE, FIN_UP, FIN_DOWN, FIN_BELOW)
+    out_low2[...] = as_rows(low_column[...])
+    out_high2[...] = as_rows(high_column[...])
+    fold(red, CX - 1, 1, out_up2, 1)
+    fold(red, 0, 0, out_down2, 1)
+    start(two, FLUID_UP[1], FLUID_DOWN[1], FLUID_SIDE[1], FLUID_ABOVE, FLUID_BELOW)
+
+    arrived(one, FIN_SIDE, FIN_UP, FIN_DOWN, FIN_BELOW, FIN_ABOVE)
 
     def fin_step(group, carry):
         low = high = jnp.zeros((8, FH), F32)
@@ -339,53 +440,8 @@
         out_fin_high2[group] = high
         return carry
 
-    lax.fori_loop(1, FD // 8, fin_step, 0)
-
-    arrived(one, FIN_ABOVE)
-
-    @pl.when(on_wall)
-    def _():
-        cells = (ROWS, CY)
-        least = (2 * FH * iota(cells, 0) + 2 * iota(cells, 1)).astype(F32)
-        roots = fin_v[1]
-        surface = []
-        for di in range(2):
-            for dj in range(2):
-                columns = dot(roots, spread(FH, CY, dj, 0))
-                surface.append(dot(spread(ROWS, FW, di, 1), columns))
-        shifts = (0.0, 1.0, float(FH), float(FH + 1))
-
-        def owned(k, sums):
-            offset = wall_in[k, ROWS:] - least
-            temps = wall_in[k, :ROWS]
-            value = jnp.zeros(cells, F32)
-            new = []
-            for part, shift, total in zip(surface, shifts, sums):
-                hit = offset == shift
-                value = jnp.where(hit, part, value)
-                new.append(total + jnp.where(hit, temps - part, 0.0))
-            back_out[k] = value
-            return tuple(new)
-
-        def step(k, sums):
-            wall_link(k).wait_recv()
-            sums = owned(k, sums)
-            back_link(k).start()
-            return sums
-
-        sums = owned(0, (jnp.zeros(cells, F32),) * 4)
-        sums = lax.fori_loop(1, blocks, step, sums)
-        deposit = jnp.zeros((FW, FH), F32)
-        for di in range(2):
-            rows = spread(FW, ROWS, di, 0)
-            for dj in range(2):
-                deposit = deposit + dot(
-                    dot(rows, sums[2 * di + dj]), spread(CY, FH, dj, 1)
-                )
-        fin_v[0] = deposit
-        first[0] = deposit
-
-    fin_step(0, 0)
+    lax.fori_loop(0, FD // 8, fin_step, 0)
+    start(two, FIN_UP, FIN_DOWN, FIN_SIDE, FIN_ABOVE, FIN_BELOW)
 
     @pl.when(on_wall)
     def _():
@@ -394,8 +450,8 @@
             return total + back_in[k]
 
         ghost = lax.fori_loop(1, blocks, step, back_out[0])
-        square = jnp.concatenate([ghost, jnp.zeros((CY - ROWS, CY), F32)], axis=0)
-        low2[...] = jnp.transpose(square)
+        in_low2[...] = ghost
+        low2[...] = as_columns(ghost)
 
         def fix(x, carry):
             lane = iota((CY, 128), 1)
@@ -407,8 +463,9 @@
 
         lax.fori_loop(0, CX, fix, 0)
 
-    start(two, FLUID_UP, FLUID_DOWN, FLUID_SIDE, FLUID_ABOVE, FLUID_BELOW,
-          FIN_UP, FIN_DOWN, FIN_SIDE, FIN_ABOVE, FIN_BELOW)
+    fold(red, CX - 1, 1, out_up2, 0)
+    fold(red, 0, 0, out_down2, 0)
+    start(two, FLUID_UP[0], FLUID_DOWN[0], FLUID_SIDE[0])
 
     sent(one)
 
@@ -422,6 +479,9 @@
         lax.fori_loop(1, blocks, step, 0)
 
     arrived(two, *range(FACES))
+    low2[...] = as_columns(in_low2[...])
+    high2[...] = as_columns(in_high2[...])
+    unfold(in_up2, in_down2, red)
     sent(two)
 
 
@@ -482,6 +542,10 @@
         pltpu.VMEM((CX, CY, CZ), jnp.int32) if s is None else pltpu.VMEM(s, F32) for s in shapes
     ]
     dma = pltpu.SemaphoreType.DMA
+    in_hbm = [
+        pltpu.with_memory_space_constraint(x, pltpu.HBM)
+        for x in (fluid_temp, active, fin_temp, fin_source)
+    ]
     middle = pl.pallas_call(
         functools.partial(exchange_kernel, sizes),
         name="exchange_and_first_sweeps",
@@ -496,8 +560,11 @@
             pltpu.VMEM((CX, CY), jnp.int32),
             pltpu.VMEM((CX, 8, CZ), F32),
             *[pltpu.VMEM(s, F32) for s in (column, column, rows, rows, strip)],
-            *[pltpu.VMEM(s, F32) for s in (column, column, rows, rows, strip)],
-            *[pltpu.VMEM(s, F32) for s in (column, column, rows, rows, strip)],
+            *[pltpu.VMEM(s, F32) for s in (rows, rows, strip)],
+            *[pltpu.VMEM(s, F32) for s in (rows, rows, strip)],
+            *[pltpu.VMEM(column, F32) for _ in range(2)],
+            *[pltpu.VMEM((ROWS, CY), F32) for _ in range(8)],
+            *[pltpu.VMEM((2, HALF, 128), F32) for _ in range(8)],
             pltpu.VMEM((blocks, 2 * ROWS, CY), F32),
             pltpu.VMEM((blocks, 2 * ROWS, CY), F32),
             pltpu.VMEM((blocks, ROWS, CY), F32),
@@ -509,7 +576,7 @@
         compiler_params=pltpu.CompilerParams(
             collective_id=0, has_side_effects=True, vmem_limit_bytes=40 * 2**20
         ),
-    )(fluid_temp, active, fin_temp, fin_source, owner, target)
+    )(*in_hbm, owner, target)
     return pl.pallas_call(
         second_kernel,
         name="second_sweeps",

time: 52.3 us -> 40.1 us (0.77)
  the two profiles are of different devices: /device:TPU:32 before, /device:TPU:2 now
where the time goes in v2:
time: 40.1 us; the launch traced here: 39.9 us
  Pallas kernels  37.9 us (95%)
  local copies, waits for them, and re-layouts  1.39 us (3%)
  between operations  0.65 us (2%)
    pallas_call x1, Pallas kernels, local(): pl.pallas_call(functools.partial(exchange_kernel, sizes), name='exchange_...  31.9 us
    pallas_call x1, Pallas kernels, local(): pl.pallas_call(second_kernel, name='second_sweeps', out_shape=[jax.ShapeD...  6.04 us
    unnamed x4, local copies, waits for them, and re-layouts  1.39 us

profile of v2, /device:TPU:2, one launch (start us, length us, event | category | flops | bytes accessed | tf_op | source)
XLA Modules:
  0.0 39.9 jit_solution(7517093059295883707)
XLA Ops:
  0.6 0.0 copy-start
  0.6 0.7 %copy-done = s32[1,1,2048,1]{2,3,1,0:T(1,128)S(1)} copy-done((s32[1,1,2048,1]{2,3,1,0:T(1,128)S(1)}, s32[1,1,2048,1]{2,3,1,0:T(1,128)}, u32[]{:S(2)}) %copy-start) | copy-done | bytes 8216
  1.3 0.0 copy-start.1
  1.3 0.7 %copy-done.1 = s32[1,1,2048]{2,1,0:T(1,128)S(1)} copy-done((s32[1,1,2048]{2,1,0:T(1,128)S(1)}, s32[1,1,2048]{2,1,0:T(1,128)}, u32[]{:S(2)}) %copy-start.1) | copy-done | bytes 8216
  2.0 31.9 %exchange_and_first_sweeps.1 = (f32[18,128,256]{2,1,0:T(8,128)S(1)}, s32[16,128,256]{2,1,0:T(8,128)S(1)}, f32[66,32,256]{2,1,0:T(8,128)S(1)}, f32[64,32,256]{2,1...) custom-call(f32[16,128,256]{2,1,0:T(8,128)} %fluid.1, ...), custom_call_target="tpu_custom_call" | custom-call | tf_op jit(solution)/shard_map/exchange_and_first_sweeps/pallas_call | solution.py:549
  33.9 6.0 %second_sweeps.1 = (f32[16,128,256]{2,1,0:T(8,128)}, f32[64,32,256]{2,1,0:T(8,128)}) custom-call(f32[18,128,256]{2,1,0:T(8,128)S(1)} %get-tuple-element.12.red, s32[16,128,256]{2,1,0:T(8,128)S(1)} %get-tuple-element.13.active, f32[66,32,256]{2,1,0:T(8,128)S(1)} %get-tuple-element.14.first, f32[64,32,256]{2,1,0:T(8,128)S(1)} %get-tuple-element.15.base, ...), custom_call_target="tpu_custom_call" | custom-call | tf_op jit(solution)/shard_map/second_sweeps/pallas_call | solution.py:580
Async XLA Ops:
  0.6 0.7 %copy-start = (s32[1,1,2048,1]{2,3,1,0:T(1,128)S(1)}, s32[1,1,2048,1]{2,3,1,0:T(1,128)}, u32[]{:S(2)}) copy-start(s32[1,1,2048,1]{2,3,1,0:T(1,128)} %param.10) | copy-start | bytes 24580
  1.3 0.7 %copy-start.1 = (s32[1,1,2048]{2,1,0:T(1,128)S(1)}, s32[1,1,2048]{2,1,0:T(1,128)}, u32[]{:S(2)}) copy-start(s32[1,1,2048]{2,1,0:T(1,128)} %param.11) | copy-start | bytes 24580

commit v3 on v2

--- a/solution.py
+++ b/solution.py
@@ -19,6 +19,8 @@
 ROWS = CX
 
 HALF = CY // 2
+PAIRS = CX // 2
+CHUNK = 32
 
 FLUID_UP, FLUID_DOWN, FLUID_SIDE = (0, 1), (2, 3), (4, 5)
 FLUID_ABOVE, FLUID_BELOW = 6, 7
@@ -56,18 +58,35 @@
     return jnp.concatenate([first, last], axis=1)
 
 
-def fluid_plane(x, field, active, side, low, high, parity, core):
-    here = field[x + 1]
-    total = field[x] + field[x + 2]
-    tile = side[x]
-    low_tile = jnp.where(core == 1, pltpu.roll(tile, 1, 0), 0.0)
-    high_tile = jnp.where(core == 0, pltpu.roll(tile, 7, 0), 0.0)
-    total = total + shifted_rows(here, low_tile, high_tile)
-    low_lane = pltpu.roll(low[...], (128 - x) % 128, 1)
-    high_lane = pltpu.roll(high[...], 127 - x, 1)
-    total = total + shifted_lanes(here, low_lane, high_lane)
-    on = jnp.where(parity_rows(here.shape) == (x + parity) % 2, active[x], 0) == 1
-    return jnp.where(on, (here + total) * SEVENTH, here)
+def half_sweep(pair, source, target, active, side, low, high, red, core, put):
+    x = 2 * pair
+    for start in range(0, CY, CHUNK):
+        rows = slice(start, start + CHUNK)
+        even = parity_rows((CHUNK, CZ)) == 0
+        here = source[pair + 1, rows]
+        before, after = source[pair, rows], source[pair + 2, rows]
+        near, far = active[x, rows], active[x + 1, rows]
+        if red:
+            total = here + jnp.where(even, before, after)
+            on = jnp.where(even, near, far) == 1
+        else:
+            total = here + jnp.where(even, after, before)
+            on = jnp.where(even, far, near) == 1
+        if start == 0:
+            low_tile = jnp.where(core == 1, pltpu.roll(side[pair], 1, 0), 0.0)
+        else:
+            low_tile = pltpu.roll(source[pair + 1, start - 8 : start], 1, 0)
+        stop = start + CHUNK
+        if stop == CY:
+            high_tile = jnp.where(core == 0, pltpu.roll(side[pair], 7, 0), 0.0)
+        else:
+            high_tile = pltpu.roll(source[pair + 1, stop : stop + 8], 7, 0)
+        total = total + shifted_rows(here, low_tile, high_tile)
+        low_lane = pltpu.roll(low[rows], (128 - x) % 128, 1)
+        high_lane = pltpu.roll(high[rows], 127 - x, 1)
+        total = total + shifted_lanes(here, low_lane, high_lane)
+        old = target[pair + 1, rows]
+        put(rows, here, jnp.where(on, (old + total) * SEVENTH, old))
 
 
 def fin_sum(group, k, field, low, high, side, core):
@@ -84,10 +103,14 @@
     return here, total
 
 
-def pick_columns(x, plane, low, high):
+def pick_low(x, plane, low, rows=slice(None)):
     lane = iota((plane.shape[0], 128), 1)
-    low[...] = jnp.where(lane == x, pltpu.roll(plane[:, :128], x, 1), low[...])
-    high[...] = jnp.where(lane == x, pltpu.roll(plane[:, 128:], (x + 1) % 128, 1), high[...])
+    low[rows] = jnp.where(lane == x, pltpu.roll(plane[:, :128], x, 1), low[rows])
+
+
+def pick_high(x, plane, high, rows=slice(None)):
+    lane = iota((plane.shape[0], 128), 1)
+    high[rows] = jnp.where(lane == x, pltpu.roll(plane[:, 128:], (x + 1) % 128, 1), high[rows])
 
 
 def one_colour(plane, colour):
@@ -134,9 +157,9 @@
 def exchange_kernel(
     sizes,
     fluid, active, fin, source, owner, target,
-    red, active_v, first, base, side2, low2, high2, fin_low2, fin_high2, fin_side2,
-    fluid_v, fin_v, source_v, owner_v, target_v,
-    side1, low1, high1, fin_low1, fin_high1, fin_side1,
+    red, black, active_v, base, side2, low2, high2,
+    fluid_v, fin_v, first, source_v, owner_v, target_v,
+    side1, low1, high1, fin_low1, fin_high1, fin_side1, fin_low2, fin_high2, fin_side2,
     out_fin_low1, out_fin_high1, out_fin_side1, out_fin_low2, out_fin_high2, out_fin_side2,
     low_column, high_column,
     out_low1, out_high1, in_low1, in_high1, out_low2, out_high2, in_low2, in_high2,
@@ -162,7 +185,7 @@
     loads = [
         pltpu.make_async_copy(owner, owner_v, load_sem.at[0]),
         pltpu.make_async_copy(target, target_v, load_sem.at[1]),
-        pltpu.make_async_copy(fluid, fluid_v.at[pl.ds(1, CX)], load_sem.at[2]),
+        pltpu.make_async_copy(fluid, fluid_v, load_sem.at[2]),
         pltpu.make_async_copy(fin, fin_v.at[pl.ds(1, FD)], load_sem.at[3]),
         pltpu.make_async_copy(active, active_v, load_sem.at[4]),
         pltpu.make_async_copy(source, source_v, load_sem.at[5]),
@@ -203,15 +226,15 @@
 
     @pl.when(jnp.logical_not(has_low))
     def _():
-        fluid_v[0] = jnp.zeros((CY, CZ), F32)
+        black[0] = jnp.zeros((CY, CZ), F32)
         red[0] = jnp.zeros((CY, CZ), F32)
         fin_low1[...] = jnp.zeros(fin_low1.shape, F32)
         fin_low2[...] = jnp.zeros(fin_low2.shape, F32)
 
     @pl.when(jnp.logical_not(has_high))
     def _():
-        fluid_v[CX + 1] = jnp.zeros((CY, CZ), F32)
-        red[CX + 1] = jnp.zeros((CY, CZ), F32)
+        black[PAIRS + 1] = jnp.zeros((CY, CZ), F32)
+        red[PAIRS + 1] = jnp.zeros((CY, CZ), F32)
         fin_high1[...] = jnp.zeros(fin_high1.shape, F32)
         fin_high2[...] = jnp.zeros(fin_high2.shape, F32)
 
@@ -229,24 +252,35 @@
     for ref in (low_column, high_column, out_fin_side1, out_fin_side2):
         ref[...] = jnp.zeros(ref.shape, F32)
 
+    loads[2].wait()
+
+    def pack_fluid(pair, carry):
+        x = 2 * pair
+        for start in range(0, CY, CHUNK):
+            rows = slice(start, start + CHUNK)
+            even = parity_rows((CHUNK, CZ)) == 0
+            near, far = fluid_v[x, rows], fluid_v[x + 1, rows]
+            reds, blacks = jnp.where(even, near, far), jnp.where(even, far, near)
+            red[pair + 1, rows] = reds
+            black[pair + 1, rows] = blacks
+            pick_low(x, blacks, low_column, rows)
+            pick_low(x + 1, reds, low_column, rows)
+            pick_high(x, blacks, high_column, rows)
+        return carry
+
+    lax.fori_loop(0, PAIRS, pack_fluid, 0)
+    out_low1[...] = as_rows(low_column[...])
+    out_high1[...] = as_rows(high_column[...])
+
+    def fold(field, pair, colour, out, half):
+        out[half] = one_colour(field[pair + 1, :, half * 128 : half * 128 + 128], colour)
+
+    for half in range(2):
+        fold(black, PAIRS - 1, 0, out_up1, half)
+        fold(black, 0, 1, out_down1, half)
+
     loads[0].wait()
     loads[1].wait()
-    loads[2].wait()
-
-    def pack_fluid(x, carry):
-        pick_columns(x, fluid_v[x + 1], low_column, high_column)
-        return carry
-
-    lax.fori_loop(0, CX, pack_fluid, 0)
-    out_low1[...] = as_rows(low_column[...])
-    out_high1[...] = as_rows(high_column[...])
-
-    def fold(field, x, colour, out, half):
-        out[half] = one_colour(field[x + 1, :, half * 128 : half * 128 + 128], colour)
-
-    for half in range(2):
-        fold(fluid_v, CX - 1, 0, out_up1, half)
-        fold(fluid_v, 0, 1, out_down1, half)
 
     expected = 1 + has_above.astype(jnp.int32) + has_below.astype(jnp.int32)
     sides = has_low.astype(jnp.int32) + has_high.astype(jnp.int32)
@@ -266,7 +300,11 @@
 
     @pl.when(on_wall)
     def _():
-        temps = out_low1[...]
+        mixed = out_low1[...]
+        swapped = jnp.where(
+            iota(mixed.shape, 0) % 2 == 0, pltpu.roll(mixed, ROWS - 1, 0), pltpu.roll(mixed, 1, 0)
+        )
+        temps = jnp.where(iota(mixed.shape, 1) % 2 == 0, swapped, mixed)
         owners = owner_v[...]
         targets = target_v[...].astype(F32)
 
@@ -298,7 +336,7 @@
         for half in range(2):
             up, down, across = FLUID_UP[half], FLUID_DOWN[half], FLUID_SIDE[half]
             lanes = pl.ds(half * 128, 128)
-            rim = side_from.at[pl.ds(1, CX), pl.ds(side_row, 8), lanes]
+            rim = side_from.at[pl.ds(1, PAIRS), pl.ds(side_row, 8), lanes]
             links[up] = (link(out_up.at[half], in_up.at[half], send, recv, up, right), has_high, has_low)
             links[down] = (link(out_down.at[half], in_down.at[half], send, recv, down, left), has_low, has_high)
             links[across] = (link(rim, side.at[:, :, lanes], send, recv, across, other), None, None)
@@ -310,7 +348,7 @@
         else:
             pl.when(condition)(action)
 
-    one = faces(send1, recv1, fluid_v, out_up1, in_up1, out_down1, in_down1, side1, out_low1, in_low1, out_high1, in_high1,
+    one = faces(send1, recv1, black, out_up1, in_up1, out_down1, in_down1, side1, out_low1, in_low1, out_high1, in_high1,
                 fin_v, fin_v, fin_low1, fin_high1, fin_side1, out_fin_low1, out_fin_high1, out_fin_side1)
     two = faces(send2, recv2, red, out_up2, in_up2, out_down2, in_down2, side2, out_low2, in_low2, out_high2, in_high2,
                 first, first, fin_low2, fin_high2, fin_side2, out_fin_low2, out_fin_high2, out_fin_side2)
@@ -351,13 +389,16 @@
     low1[...] = as_columns(in_low1[...])
     high1[...] = as_columns(in_high1[...])
 
-    def red_step(x, carry):
-        new = fluid_plane(x, fluid_v, active_v, side1, low1, high1, 0, core)
-        red[x + 1] = new
-        pick_columns(x, new, low_column, high_column)
+    def red_step(pair, carry):
+        def put(rows, sources, new):
+            red[pair + 1, rows] = new
+            pick_low(2 * pair, new, low_column, rows)
+            pick_high(2 * pair, new, high_column, rows)
+
+        half_sweep(pair, black, red, active_v, side1, low1, high1, True, core, put)
         return carry
 
-    lax.fori_loop(1, CX - 1, red_step, 0)
+    lax.fori_loop(1, PAIRS - 1, red_step, 0)
 
     @pl.when(on_wall)
     def _():
@@ -408,18 +449,18 @@
 
         def high_plane():
             for half in range(2):
-                field[CX + 1, :, half * 128 : half * 128 + 128] = both_halves(arrived_down[half])
+                field[PAIRS + 1, :, half * 128 : half * 128 + 128] = both_halves(arrived_down[half])
 
         when(has_low, low_plane)
         when(has_high, high_plane)
 
     arrived(one, *FLUID_UP, *FLUID_DOWN)
-    unfold(in_up1, in_down1, fluid_v)
+    unfold(in_up1, in_down1, black)
     red_step(0, 0)
-    red_step(CX - 1, 0)
+    red_step(PAIRS - 1, 0)
     out_low2[...] = as_rows(low_column[...])
     out_high2[...] = as_rows(high_column[...])
-    fold(red, CX - 1, 1, out_up2, 1)
+    fold(red, PAIRS - 1, 1, out_up2, 1)
     fold(red, 0, 0, out_down2, 1)
     start(two, FLUID_UP[1], FLUID_DOWN[1], FLUID_SIDE[1], FLUID_ABOVE, FLUID_BELOW)
 
@@ -450,20 +491,24 @@
             return total + back_in[k]
 
         ghost = lax.fori_loop(1, blocks, step, back_out[0])
-        in_low2[...] = ghost
-        low2[...] = as_columns(ghost)
-
-        def fix(x, carry):
+        later = pltpu.roll(ghost, ROWS - 1, 0)
+        even_cell = iota(ghost.shape, 1) % 2 == 0
+        in_low2[...] = jnp.where(even_cell, later, ghost)
+        low2[...] = as_columns(jnp.where(even_cell, ghost, later))
+
+        def fix(pair, carry):
+            x = 2 * pair
             lane = iota((CY, 128), 1)
-            on = jnp.where(parity_rows((CY, 128)) == x % 2, active_v[x, :, :128], 0) == 1
+            even = parity_rows((CY, 128)) == 0
+            on = jnp.where(even, active_v[x, :, :128], active_v[x + 1, :, :128]) == 1
             share = pltpu.roll(low2[...], (128 - x) % 128, 1) * SEVENTH
-            half = red[x + 1, :, :128]
-            red[x + 1, :, :128] = half + jnp.where(on & (lane == 0), share, 0.0)
+            half = red[pair + 1, :, :128]
+            red[pair + 1, :, :128] = half + jnp.where(on & (lane == 0), share, 0.0)
             return carry
 
-        lax.fori_loop(0, CX, fix, 0)
-
-    fold(red, CX - 1, 1, out_up2, 0)
+        lax.fori_loop(0, PAIRS, fix, 0)
+
+    fold(red, PAIRS - 1, 1, out_up2, 0)
     fold(red, 0, 0, out_down2, 0)
     start(two, FLUID_UP[0], FLUID_DOWN[0], FLUID_SIDE[0])
 
@@ -478,53 +523,51 @@
 
         lax.fori_loop(1, blocks, step, 0)
 
-    arrived(two, *range(FACES))
+    arrived(two, FIN_UP, FIN_DOWN, FIN_SIDE, FIN_ABOVE, FIN_BELOW)
+
+    def fin_again(group, carry):
+        for k in range(8):
+            d = group * 8 + k
+            _, total = fin_sum(group, k, first, fin_low2, fin_high2, fin_side2, core)
+            base[d] = base[d] + (OMEGA * SEVENTH) * total
+        return carry
+
+    lax.fori_loop(0, FD // 8, fin_again, 0)
+
+    arrived(two, *FLUID_UP, *FLUID_DOWN, *FLUID_SIDE, FLUID_ABOVE, FLUID_BELOW)
     low2[...] = as_columns(in_low2[...])
     high2[...] = as_columns(in_high2[...])
     unfold(in_up2, in_down2, red)
     sent(two)
 
 
-def second_kernel(
-    red, active, first, base, side, low, high, fin_low, fin_high, fin_side,
-    fluid_out, fin_out, fluid_v, fin_v, fluid_sem, fin_sem,
-):
+def second_kernel(red, black, active, fin_new, side, low, high, fluid_out, fin_out, fluid_v, fluid_sem, fin_sem):
     core = lax.axis_index("gy")
-
-    def fluid_copy(x):
-        return pltpu.make_async_copy(fluid_v.at[x], fluid_out.at[x], fluid_sem.at[x])
-
-    def fin_copy(group):
-        part = pl.ds(group * 8, 8)
-        return pltpu.make_async_copy(fin_v.at[part], fin_out.at[part], fin_sem.at[group])
-
-    def black_step(x, carry):
-        fluid_v[x] = fluid_plane(x, red, active, side, low, high, 1, core)
-        fluid_copy(x).start()
+    fin_copy = pltpu.make_async_copy(fin_new, fin_out, fin_sem)
+    fin_copy.start()
+
+    def fluid_copy(pair):
+        planes = pl.ds(2 * pair, 2)
+        return pltpu.make_async_copy(fluid_v.at[planes], fluid_out.at[planes], fluid_sem.at[pair])
+
+    def black_step(pair, carry):
+        def put(rows, reds, new):
+            even = parity_rows(new.shape) == 0
+            fluid_v[2 * pair, rows] = jnp.where(even, reds, new)
+            fluid_v[2 * pair + 1, rows] = jnp.where(even, new, reds)
+
+        half_sweep(pair, red, black, active, side, low, high, False, core, put)
+        fluid_copy(pair).start()
         return carry
 
-    lax.fori_loop(0, CX, black_step, 0)
-
-    def fin_step(group, carry):
-        for k in range(8):
-            d = group * 8 + k
-            _, total = fin_sum(group, k, first, fin_low, fin_high, fin_side, core)
-            fin_v[d] = base[d] + (OMEGA * SEVENTH) * total
-        fin_copy(group).start()
+    lax.fori_loop(0, PAIRS, black_step, 0)
+
+    def done(pair, carry):
+        fluid_copy(pair).wait()
         return carry
 
-    lax.fori_loop(0, FD // 8, fin_step, 0)
-
-    def fluid_done(x, carry):
-        fluid_copy(x).wait()
-        return carry
-
-    def fin_done(group, carry):
-        fin_copy(group).wait()
-        return carry
-
-    lax.fori_loop(0, CX, fluid_done, 0)
-    lax.fori_loop(0, FD // 8, fin_done, 0)
+    lax.fori_loop(0, PAIRS, done, 0)
+    fin_copy.wait()
 
 
 def local(sizes, fluid_temp, active, fin_temp, fin_source, wall_owner, wall_target):
@@ -534,32 +577,33 @@
     anywhere = pl.BlockSpec(memory_space=pl.ANY)
     vmem = pl.BlockSpec(memory_space=pltpu.VMEM)
     column, rows, strip = (CY, 128), (FD // 8, 8, FH), (FW, 128)
-    shapes = [
-        (CX + 2, CY, CZ), None, (FD + 2, FW, FH), (FD, FW, FH),
-        (CX, 8, CZ), column, column, rows, rows, strip,
-    ]
+    packed, rim = (PAIRS + 2, CY, CZ), (PAIRS, 8, CZ)
     held = [
-        pltpu.VMEM((CX, CY, CZ), jnp.int32) if s is None else pltpu.VMEM(s, F32) for s in shapes
+        pltpu.VMEM(packed, F32),
+        pltpu.VMEM(packed, F32),
+        pltpu.VMEM((CX, CY, CZ), jnp.int32),
+        *[pltpu.VMEM(s, F32) for s in ((FD, FW, FH), rim, column, column)],
     ]
     dma = pltpu.SemaphoreType.DMA
     in_hbm = [
         pltpu.with_memory_space_constraint(x, pltpu.HBM)
-        for x in (fluid_temp, active, fin_temp, fin_source)
+        for x in (fluid_temp, active, fin_temp, fin_source, owner, target)
     ]
     middle = pl.pallas_call(
         functools.partial(exchange_kernel, sizes),
         name="exchange_and_first_sweeps",
         out_shape=held,
         in_specs=[anywhere] * 6,
-        out_specs=[vmem] * 10,
+        out_specs=[vmem] * 7,
         scratch_shapes=[
-            pltpu.VMEM((CX + 2, CY, CZ), F32),
+            pltpu.VMEM((CX, CY, CZ), F32),
+            pltpu.VMEM((FD + 2, FW, FH), F32),
             pltpu.VMEM((FD + 2, FW, FH), F32),
             pltpu.VMEM((FD, FW, FH), F32),
             pltpu.VMEM((CX, CY), jnp.int32),
             pltpu.VMEM((CX, CY), jnp.int32),
-            pltpu.VMEM((CX, 8, CZ), F32),
-            *[pltpu.VMEM(s, F32) for s in (column, column, rows, rows, strip)],
+            *[pltpu.VMEM(s, F32) for s in (rim, column, column, rows, rows, strip)],
+            *[pltpu.VMEM(s, F32) for s in (rows, rows, strip)],
             *[pltpu.VMEM(s, F32) for s in (rows, rows, strip)],
             *[pltpu.VMEM(s, F32) for s in (rows, rows, strip)],
             *[pltpu.VMEM(column, F32) for _ in range(2)],
@@ -576,7 +620,7 @@
         compiler_params=pltpu.CompilerParams(
             collective_id=0, has_side_effects=True, vmem_limit_bytes=40 * 2**20
         ),
-    )(*in_hbm, owner, target)
+    )(*in_hbm)
     return pl.pallas_call(
         second_kernel,
         name="second_sweeps",
@@ -584,13 +628,12 @@
             jax.ShapeDtypeStruct((CX, CY, CZ), F32),
             jax.ShapeDtypeStruct((FD, FW, FH), F32),
         ],
-        in_specs=[vmem] * 10,
+        in_specs=[vmem] * 7,
         out_specs=[anywhere] * 2,
         scratch_shapes=[
             pltpu.VMEM((CX, CY, CZ), F32),
-            pltpu.VMEM((FD, FW, FH), F32),
-            dma((CX,)),
-            dma((FD // 8,)),
+            dma((PAIRS,)),
+            dma,
         ],
         compiler_params=pltpu.CompilerParams(vmem_limit_bytes=40 * 2**20),
     )(*middle)

time: 40.1 us -> 35.8 us (0.89)
  Pallas kernels: 37.9 us -> 34.7 us
  local copies, waits for them, and re-layouts: 1.39 us -> 0 us
    pallas_call x1, Pallas kernels: 6.04 us -> 2.22 us  [local(): pl.pallas_call(second_kernel, name='second_sweeps', out_shape=[jax.ShapeD...]
    unnamed x4 -> x0, local copies, waits for them, and re-layouts: 1.39 us -> none
    pallas_call x1, Pallas kernels: 31.9 us -> 32.5 us  [local(): pl.pallas_call(functools.partial(exchange_kernel, sizes), name='exchange_...]
where the time goes in v3:
time: 35.8 us; the launch traced here: 35.4 us
  Pallas kernels  34.7 us (97%)
  between operations  0.64 us (2%)
    pallas_call x1, Pallas kernels, local(): pl.pallas_call(functools.partial(exchange_kernel, sizes), name='exchange_...  32.5 us
    pallas_call x1, Pallas kernels, local(): pl.pallas_call(second_kernel, name='second_sweeps', out_shape=[jax.ShapeD...  2.22 us

profile of v3, /device:TPU:2, one launch (start us, length us, event | category | flops | bytes accessed | tf_op | source)
XLA Modules:
  0.0 35.4 jit_solution(3419712754660504731)
XLA Ops:
  0.6 32.5 %exchange_and_first_sweeps.1 = (f32[10,128,256]{2,1,0:T(8,128)S(1)}, f32[10,128,256]{2,1,0:T(8,128)S(1)}, s32[16,128,256]{2,1,0:T(8,128)S(1)}, f32[64,32,256]{2,...) custom-call(f32[16,128,256]{2,1,0:T(8,128)} %fluid.1, ...), custom_call_target="tpu_custom_call" | custom-call | tf_op jit(solution)/shard_map/exchange_and_first_sweeps/pallas_call | solution.py:592
  33.2 2.2 %second_sweeps.1 = (f32[16,128,256]{2,1,0:T(8,128)}, f32[64,32,256]{2,1,0:T(8,128)}) custom-call(f32[10,128,256]{2,1,0:T(8,128)S(1)} %get-tuple-element.9.red, f32[10,128,256]{2,1,0:T(8,128)S(1)} %get-tuple-element.10.black, s32[16,128,256]{2,1,0:T(8,128)S(1)} %get-tuple-element.11.active, f32[64,32,256]{2,1,0:T(8,128)S(1)} %get-tuple-element.12.fin_new, ...), custom_call_target="tpu_custom_call" | custom-call | tf_op jit(solution)/shard_map/second_sweeps/pallas_call | solution.py:624

commit v4 on v3

--- a/solution.py
+++ b/solution.py
@@ -164,8 +164,8 @@
     low_column, high_column,
     out_low1, out_high1, in_low1, in_high1, out_low2, out_high2, in_low2, in_high2,
     out_up1, out_down1, in_up1, in_down1, out_up2, out_down2, in_up2, in_down2,
-    wall_out, wall_in, back_out, back_in,
-    load_sem, send1, recv1, send2, recv2, wall_send, wall_recv, back_send, back_recv,
+    wall_out, wall_in, temps_out, temps_in, back_out, back_in, surface,
+    load_sem, send1, recv1, send2, recv2, wall_send, wall_recv, temps_send, temps_recv, back_send, back_recv,
 ):
     groups, blocks = sizes
     grp, gx, core = lax.axis_index("grp"), lax.axis_index("gx"), lax.axis_index("gy")
@@ -176,20 +176,22 @@
     below, above = (grp - 1, gx, core), (grp + 1, gx, core)
     other = (grp, gx, 1 - core)
 
+    def wrapped(index):
+        return jnp.where(index >= blocks, index - blocks, index)
+
     def peer(k):
-        return (grp, lax.rem(gx + k, blocks), core)
+        return (grp, wrapped(gx + k), core)
 
     def peer_back(k):
-        return (grp, lax.rem(gx - k + blocks, blocks), core)
-
-    loads = [
-        pltpu.make_async_copy(owner, owner_v, load_sem.at[0]),
-        pltpu.make_async_copy(target, target_v, load_sem.at[1]),
-        pltpu.make_async_copy(fluid, fluid_v, load_sem.at[2]),
-        pltpu.make_async_copy(fin, fin_v.at[pl.ds(1, FD)], load_sem.at[3]),
-        pltpu.make_async_copy(active, active_v, load_sem.at[4]),
-        pltpu.make_async_copy(source, source_v, load_sem.at[5]),
-    ]
+        return (grp, wrapped(gx - k + blocks), core)
+
+    load_owner = pltpu.make_async_copy(owner, owner_v, load_sem.at[0])
+    load_target = pltpu.make_async_copy(target, target_v, load_sem.at[1])
+    load_fin = pltpu.make_async_copy(fin, fin_v.at[pl.ds(1, FD)], load_sem.at[2])
+    load_fluid = pltpu.make_async_copy(fluid, fluid_v, load_sem.at[3])
+    load_source = pltpu.make_async_copy(source, source_v, load_sem.at[4])
+    load_active = pltpu.make_async_copy(active, active_v, load_sem.at[5])
+    loads = (load_owner, load_target, load_fin, load_fluid, load_source, load_active)
     for load in loads:
         load.start()
 
@@ -252,35 +254,21 @@
     for ref in (low_column, high_column, out_fin_side1, out_fin_side2):
         ref[...] = jnp.zeros(ref.shape, F32)
 
-    loads[2].wait()
-
-    def pack_fluid(pair, carry):
-        x = 2 * pair
-        for start in range(0, CY, CHUNK):
-            rows = slice(start, start + CHUNK)
-            even = parity_rows((CHUNK, CZ)) == 0
-            near, far = fluid_v[x, rows], fluid_v[x + 1, rows]
-            reds, blacks = jnp.where(even, near, far), jnp.where(even, far, near)
-            red[pair + 1, rows] = reds
-            black[pair + 1, rows] = blacks
-            pick_low(x, blacks, low_column, rows)
-            pick_low(x + 1, reds, low_column, rows)
-            pick_high(x, blacks, high_column, rows)
+    load_fin.wait()
+
+    def pack_fin(group, carry):
+        low = high = jnp.zeros((8, FH), F32)
+        for k in range(8):
+            plane = fin_v[group * 8 + k + 1]
+            low, high = pick_rows(k, plane, low, high)
+            pick_side(group * 8 + k, plane, out_fin_side1, core)
+        out_fin_low1[group] = low
+        out_fin_high1[group] = high
         return carry
 
-    lax.fori_loop(0, PAIRS, pack_fluid, 0)
-    out_low1[...] = as_rows(low_column[...])
-    out_high1[...] = as_rows(high_column[...])
-
-    def fold(field, pair, colour, out, half):
-        out[half] = one_colour(field[pair + 1, :, half * 128 : half * 128 + 128], colour)
-
-    for half in range(2):
-        fold(black, PAIRS - 1, 0, out_up1, half)
-        fold(black, 0, 1, out_down1, half)
-
-    loads[0].wait()
-    loads[1].wait()
+    lax.fori_loop(0, FD // 8, pack_fin, 0)
+    load_owner.wait()
+    load_target.wait()
 
     expected = 1 + has_above.astype(jnp.int32) + has_below.astype(jnp.int32)
     sides = has_low.astype(jnp.int32) + has_high.astype(jnp.int32)
@@ -298,26 +286,23 @@
     def back_link(k):
         return link(back_out.at[k], back_in.at[k], back_send, back_recv, k, peer_back(k))
 
+    def temps_link(k):
+        return link(temps_out, temps_in.at[k], temps_send, temps_recv, k, peer(k))
+
     @pl.when(on_wall)
     def _():
-        mixed = out_low1[...]
-        swapped = jnp.where(
-            iota(mixed.shape, 0) % 2 == 0, pltpu.roll(mixed, ROWS - 1, 0), pltpu.roll(mixed, 1, 0)
-        )
-        temps = jnp.where(iota(mixed.shape, 1) % 2 == 0, swapped, mixed)
         owners = owner_v[...]
         targets = target_v[...].astype(F32)
 
-        def masked(k, out):
-            out[k, :ROWS] = temps
-            out[k, ROWS:] = jnp.where(owners == lax.rem(gx + k, blocks), targets, -1.0)
+        def owned_by(k):
+            return jnp.where(owners == wrapped(gx + k), targets, -1.0)
 
         def step(k, carry):
-            masked(k, wall_out)
+            wall_out[k] = owned_by(k)
             wall_link(k).start()
             return carry
 
-        masked(0, wall_in)
+        wall_in[0] = owned_by(0)
         lax.fori_loop(1, blocks, step, 0)
 
     side_row = pl.multiple_of(jnp.where(core == 0, CY - 8, 0), 8)
@@ -365,105 +350,84 @@
         for k in range(FACES):
             when(links[k][1], links[k][0].wait_send)
 
+    start(one, FIN_SIDE, FIN_UP, FIN_DOWN, FIN_ABOVE, FIN_BELOW)
+
+    load_fluid.wait()
+
+    def pack_fluid(pair, carry):
+        x = 2 * pair
+        for start in range(0, CY, CHUNK):
+            rows = slice(start, start + CHUNK)
+            even = parity_rows((CHUNK, CZ)) == 0
+            near, far = fluid_v[x, rows], fluid_v[x + 1, rows]
+            reds, blacks = jnp.where(even, near, far), jnp.where(even, far, near)
+            red[pair + 1, rows] = reds
+            black[pair + 1, rows] = blacks
+            pick_low(x, blacks, low_column, rows)
+            pick_low(x + 1, reds, low_column, rows)
+            pick_high(x, blacks, high_column, rows)
+        return carry
+
+    lax.fori_loop(0, PAIRS, pack_fluid, 0)
+    out_low1[...] = as_rows(low_column[...])
+    out_high1[...] = as_rows(high_column[...])
+
+    def fold(field, pair, colour, out, half):
+        out[half] = one_colour(field[pair + 1, :, half * 128 : half * 128 + 128], colour)
+
+    for half in range(2):
+        fold(black, PAIRS - 1, 0, out_up1, half)
+        fold(black, 0, 1, out_down1, half)
+
     start(one, *FLUID_UP, *FLUID_DOWN, *FLUID_SIDE, FLUID_ABOVE, FLUID_BELOW)
 
-    loads[3].wait()
-    start(one, FIN_ABOVE, FIN_BELOW)
-
-    def pack_fin(group, carry):
-        low = high = jnp.zeros((8, FH), F32)
-        for k in range(8):
-            plane = fin_v[group * 8 + k + 1]
-            low, high = pick_rows(k, plane, low, high)
-            pick_side(group * 8 + k, plane, out_fin_side1, core)
-        out_fin_low1[group] = low
-        out_fin_high1[group] = high
-        return carry
-
-    lax.fori_loop(0, FD // 8, pack_fin, 0)
-    start(one, FIN_SIDE, FIN_UP, FIN_DOWN)
-
-    loads[4].wait()
-    loads[5].wait()
-    arrived(one, *FLUID_SIDE, FLUID_ABOVE, FLUID_BELOW)
-    low1[...] = as_columns(in_low1[...])
-    high1[...] = as_columns(in_high1[...])
-
-    def red_step(pair, carry):
-        def put(rows, sources, new):
-            red[pair + 1, rows] = new
-            pick_low(2 * pair, new, low_column, rows)
-            pick_high(2 * pair, new, high_column, rows)
-
-        half_sweep(pair, black, red, active_v, side1, low1, high1, True, core, put)
-        return carry
-
-    lax.fori_loop(1, PAIRS - 1, red_step, 0)
-
     @pl.when(on_wall)
     def _():
-        cells = (ROWS, CY)
-        least = (2 * FH * iota(cells, 0) + 2 * iota(cells, 1)).astype(F32)
+        mixed = out_low1[...]
+        swapped = jnp.where(
+            iota(mixed.shape, 0) % 2 == 0, pltpu.roll(mixed, ROWS - 1, 0), pltpu.roll(mixed, 1, 0)
+        )
+        temps = jnp.where(iota(mixed.shape, 1) % 2 == 0, swapped, mixed)
+        temps_out[...] = temps
+        temps_in[0] = temps
+
+        def step(k, carry):
+            temps_link(k).start()
+            return carry
+
+        lax.fori_loop(1, blocks, step, 0)
+
+    cells = (ROWS, CY)
+    shifts = (0.0, 1.0, float(FH), float(FH + 1))
+
+    def offsets(k):
+        return wall_in[k] - (2 * FH * iota(cells, 0) + 2 * iota(cells, 1)).astype(F32)
+
+    @pl.when(on_wall)
+    def _():
         roots = fin_v[1]
-        surface = []
+        columns = [dot(roots, spread(FH, CY, dj, 0)) for dj in range(2)]
         for di in range(2):
             for dj in range(2):
-                columns = dot(roots, spread(FH, CY, dj, 0))
-                surface.append(dot(spread(ROWS, FW, di, 1), columns))
-        shifts = (0.0, 1.0, float(FH), float(FH + 1))
-
-        def owned(k, sums):
-            offset = wall_in[k, ROWS:] - least
-            temps = wall_in[k, :ROWS]
+                surface[2 * di + dj] = dot(spread(ROWS, FW, di, 1), columns[dj])
+
+        def answer(k):
+            offset = offsets(k)
             value = jnp.zeros(cells, F32)
-            new = []
-            for part, shift, total in zip(surface, shifts, sums):
-                hit = offset == shift
-                value = jnp.where(hit, part, value)
-                new.append(total + jnp.where(hit, temps - part, 0.0))
+            for n, shift in enumerate(shifts):
+                value = jnp.where(offset == shift, surface[n], value)
             back_out[k] = value
-            return tuple(new)
-
-        def step(k, sums):
+
+        def step(k, carry):
             wall_link(k).wait_recv()
-            sums = owned(k, sums)
+            answer(k)
             back_link(k).start()
-            return sums
-
-        sums = owned(0, (jnp.zeros(cells, F32),) * 4)
-        sums = lax.fori_loop(1, blocks, step, sums)
-        deposit = jnp.zeros((FW, FH), F32)
-        for di in range(2):
-            rows = spread(FW, ROWS, di, 0)
-            for dj in range(2):
-                deposit = deposit + dot(
-                    dot(rows, sums[2 * di + dj]), spread(CY, FH, dj, 1)
-                )
-        fin_v[0] = deposit
-        first[0] = deposit
-
-    def unfold(arrived_up, arrived_down, field):
-        def low_plane():
-            for half in range(2):
-                field[0, :, half * 128 : half * 128 + 128] = both_halves(arrived_up[half])
-
-        def high_plane():
-            for half in range(2):
-                field[PAIRS + 1, :, half * 128 : half * 128 + 128] = both_halves(arrived_down[half])
-
-        when(has_low, low_plane)
-        when(has_high, high_plane)
-
-    arrived(one, *FLUID_UP, *FLUID_DOWN)
-    unfold(in_up1, in_down1, black)
-    red_step(0, 0)
-    red_step(PAIRS - 1, 0)
-    out_low2[...] = as_rows(low_column[...])
-    out_high2[...] = as_rows(high_column[...])
-    fold(red, PAIRS - 1, 1, out_up2, 1)
-    fold(red, 0, 0, out_down2, 1)
-    start(two, FLUID_UP[1], FLUID_DOWN[1], FLUID_SIDE[1], FLUID_ABOVE, FLUID_BELOW)
-
+            return carry
+
+        answer(0)
+        lax.fori_loop(1, blocks, step, 0)
+
+    load_source.wait()
     arrived(one, FIN_SIDE, FIN_UP, FIN_DOWN, FIN_BELOW, FIN_ABOVE)
 
     def fin_step(group, carry):
@@ -481,8 +445,66 @@
         out_fin_high2[group] = high
         return carry
 
-    lax.fori_loop(0, FD // 8, fin_step, 0)
+    lax.fori_loop(1, FD // 8, fin_step, 0)
+
+    @pl.when(on_wall)
+    def _():
+        def owned(k, sums):
+            offset = offsets(k)
+            flux = temps_in[k] - back_out[k]
+            return tuple(
+                total + jnp.where(offset == shift, flux, 0.0) for shift, total in zip(shifts, sums)
+            )
+
+        def step(k, sums):
+            temps_link(k).wait_recv()
+            return owned(k, sums)
+
+        sums = owned(0, (jnp.zeros(cells, F32),) * 4)
+        sums = lax.fori_loop(1, blocks, step, sums)
+        deposit = jnp.zeros((FW, FH), F32)
+        for dj in range(2):
+            rows = dot(spread(FW, ROWS, 0, 0), sums[dj]) + dot(spread(FW, ROWS, 1, 0), sums[2 + dj])
+            deposit = deposit + dot(rows, spread(CY, FH, dj, 1))
+        fin_v[0] = deposit
+        first[0] = deposit
+
+    fin_step(0, 0)
     start(two, FIN_UP, FIN_DOWN, FIN_SIDE, FIN_ABOVE, FIN_BELOW)
+
+    load_active.wait()
+    arrived(one, *FLUID_UP, *FLUID_DOWN, *FLUID_SIDE, FLUID_ABOVE, FLUID_BELOW)
+    low1[...] = as_columns(in_low1[...])
+    high1[...] = as_columns(in_high1[...])
+
+    def red_step(pair, carry):
+        def put(rows, sources, new):
+            red[pair + 1, rows] = new
+            pick_low(2 * pair, new, low_column, rows)
+            pick_high(2 * pair, new, high_column, rows)
+
+        half_sweep(pair, black, red, active_v, side1, low1, high1, True, core, put)
+        return carry
+
+    def unfold(arrived_up, arrived_down, field):
+        def low_plane():
+            for half in range(2):
+                field[0, :, half * 128 : half * 128 + 128] = both_halves(arrived_up[half])
+
+        def high_plane():
+            for half in range(2):
+                field[PAIRS + 1, :, half * 128 : half * 128 + 128] = both_halves(arrived_down[half])
+
+        when(has_low, low_plane)
+        when(has_high, high_plane)
+
+    unfold(in_up1, in_down1, black)
+    lax.fori_loop(0, PAIRS, red_step, 0)
+    out_low2[...] = as_rows(low_column[...])
+    out_high2[...] = as_rows(high_column[...])
+    fold(red, PAIRS - 1, 1, out_up2, 1)
+    fold(red, 0, 0, out_down2, 1)
+    start(two, FLUID_UP[1], FLUID_DOWN[1], FLUID_SIDE[1], FLUID_ABOVE, FLUID_BELOW)
 
     @pl.when(on_wall)
     def _():
@@ -518,6 +540,7 @@
     def _():
         def step(k, carry):
             wall_link(k).wait_send()
+            temps_link(k).wait_send()
             back_link(k).wait_send()
             return carry
 
@@ -609,13 +632,14 @@
             *[pltpu.VMEM(column, F32) for _ in range(2)],
             *[pltpu.VMEM((ROWS, CY), F32) for _ in range(8)],
             *[pltpu.VMEM((2, HALF, 128), F32) for _ in range(8)],
-            pltpu.VMEM((blocks, 2 * ROWS, CY), F32),
-            pltpu.VMEM((blocks, 2 * ROWS, CY), F32),
             pltpu.VMEM((blocks, ROWS, CY), F32),
             pltpu.VMEM((blocks, ROWS, CY), F32),
+            pltpu.VMEM((ROWS, CY), F32),
+            *[pltpu.VMEM((blocks, ROWS, CY), F32) for _ in range(3)],
+            pltpu.VMEM((4, ROWS, CY), F32),
             dma((6,)),
             *[dma((FACES,)) for _ in range(4)],
-            *[dma((blocks,)) for _ in range(4)],
+            *[dma((blocks,)) for _ in range(6)],
         ],
         compiler_params=pltpu.CompilerParams(
             collective_id=0, has_side_effects=True, vmem_limit_bytes=40 * 2**20

time: 35.8 us -> 35 us (0.978)
  Pallas kernels: 34.7 us -> 34.2 us
    pallas_call x1, Pallas kernels: 32.5 us -> 32 us  [local(): pl.pallas_call(functools.partial(exchange_kernel, sizes), name='exchange_...]
where the time goes in v4:
time: 35 us; the launch traced here: 34.9 us
  Pallas kernels  34.2 us (98%)
  between operations  0.64 us (2%)
    pallas_call x1, Pallas kernels, local(): pl.pallas_call(functools.partial(exchange_kernel, sizes), name='exchange_...  32 us
    pallas_call x1, Pallas kernels, local(): pl.pallas_call(second_kernel, name='second_sweeps', out_shape=[jax.ShapeD...  2.22 us

profile of v4, /device:TPU:2, one launch (start us, length us, event | category | flops | bytes accessed | tf_op | source)
XLA Modules:
  0.0 34.9 jit_solution(14405222883688340844)
XLA Ops:
  0.6 32.0 %exchange_and_first_sweeps.1 = (f32[10,128,256]{2,1,0:T(8,128)S(1)}, f32[10,128,256]{2,1,0:T(8,128)S(1)}, s32[16,128,256]{2,1,0:T(8,128)S(1)}, f32[64,32,256]{2,...) custom-call(f32[16,128,256]{2,1,0:T(8,128)} %fluid.1, ...), custom_call_target="tpu_custom_call" | custom-call | tf_op jit(solution)/shard_map/exchange_and_first_sweeps/pallas_call | solution.py:615
  32.7 2.2 %second_sweeps.1 = (f32[16,128,256]{2,1,0:T(8,128)}, f32[64,32,256]{2,1,0:T(8,128)}) custom-call(f32[10,128,256]{2,1,0:T(8,128)S(1)} %get-tuple-element.9.red, f32[10,128,256]{2,1,0:T(8,128)S(1)} %get-tuple-element.10.black, s32[16,128,256]{2,1,0:T(8,128)S(1)} %get-tuple-element.11.active, f32[64,32,256]{2,1,0:T(8,128)S(1)} %get-tuple-element.12.fin_new, ...), custom_call_target="tpu_custom_call" | custom-call | tf_op jit(solution)/shard_map/second_sweeps/pallas_call | solution.py:648

commit v5 on v4

--- a/solution.py
+++ b/solution.py
@@ -534,18 +534,6 @@
     fold(red, 0, 0, out_down2, 0)
     start(two, FLUID_UP[0], FLUID_DOWN[0], FLUID_SIDE[0])
 
-    sent(one)
-
-    @pl.when(on_wall)
-    def _():
-        def step(k, carry):
-            wall_link(k).wait_send()
-            temps_link(k).wait_send()
-            back_link(k).wait_send()
-            return carry
-
-        lax.fori_loop(1, blocks, step, 0)
-
     arrived(two, FIN_UP, FIN_DOWN, FIN_SIDE, FIN_ABOVE, FIN_BELOW)
 
     def fin_again(group, carry):
@@ -556,6 +544,18 @@
         return carry
 
     lax.fori_loop(0, FD // 8, fin_again, 0)
+
+    sent(one)
+
+    @pl.when(on_wall)
+    def _():
+        def step(k, carry):
+            wall_link(k).wait_send()
+            temps_link(k).wait_send()
+            back_link(k).wait_send()
+            return carry
+
+        lax.fori_loop(1, blocks, step, 0)
 
     arrived(two, *FLUID_UP, *FLUID_DOWN, *FLUID_SIDE, FLUID_ABOVE, FLUID_BELOW)
     low2[...] = as_columns(in_low2[...])

time: 35 us -> 35 us (level)
  no operation moved by 1% of the time
where the time goes in v5:
time: 35 us; the launch traced here: 34.9 us
  Pallas kernels  34.2 us (98%)
  between operations  0.64 us (2%)
    pallas_call x1, Pallas kernels, local(): pl.pallas_call(functools.partial(exchange_kernel, sizes), name='exchange_...  32 us
    pallas_call x1, Pallas kernels, local(): pl.pallas_call(second_kernel, name='second_sweeps', out_shape=[jax.ShapeD...  2.22 us

profile of v5, /device:TPU:2, one launch (start us, length us, event | category | flops | bytes accessed | tf_op | source)
XLA Modules:
  0.0 34.9 jit_solution(17517668554871743731)
XLA Ops:
  0.6 32.0 %exchange_and_first_sweeps.1 = (f32[10,128,256]{2,1,0:T(8,128)S(1)}, f32[10,128,256]{2,1,0:T(8,128)S(1)}, s32[16,128,256]{2,1,0:T(8,128)S(1)}, f32[64,32,256]{2,...) custom-call(f32[16,128,256]{2,1,0:T(8,128)} %fluid.1, ...), custom_call_target="tpu_custom_call" | custom-call | tf_op jit(solution)/shard_map/exchange_and_first_sweeps/pallas_call | solution.py:615
  32.7 2.2 %second_sweeps.1 = (f32[16,128,256]{2,1,0:T(8,128)}, f32[64,32,256]{2,1,0:T(8,128)}) custom-call(f32[10,128,256]{2,1,0:T(8,128)S(1)} %get-tuple-element.9.red, f32[10,128,256]{2,1,0:T(8,128)S(1)} %get-tuple-element.10.black, s32[16,128,256]{2,1,0:T(8,128)S(1)} %get-tuple-element.11.active, f32[64,32,256]{2,1,0:T(8,128)S(1)} %get-tuple-element.12.fin_new, ...), custom_call_target="tpu_custom_call" | custom-call | tf_op jit(solution)/shard_map/second_sweeps/pallas_call | solution.py:648
